TPU v7x, 32 devices: a whole 2x2x4 slice. The times are simulated.
32 devices in a mesh: ply: 2 (over x), gx: 4 (over y, core), gy: 4 (over z).
Axes of the slice: x: 2, y: 2, z: 4, core: 2. Of those that a mesh axis runs over, the one named last changes fastest.
Arguments:
- coords: float32 [3, 2, 24, 24, 128], P(None, 'ply', 'gx', 'gy'), may hold values from 0 to 1
- strain: float32 [2, 24, 24, 128], P('ply', 'gx', 'gy'), may hold values from 0.1 to 10.1
- kappa_old: float32 [2, 24, 24, 128], P('ply', 'gx', 'gy'), may hold values from 1 to 3
- counts: int32 [2, 24, 24], P('ply', 'gx', 'gy'), may hold values from 0 to 128, as said below
- pair_mask: int32 [2, 24, 24, 26], P('ply', 'gx', 'gy'), may hold values from 0 to 1, as said below
Outputs:
- kappa_new: float32 [2, 24, 24, 128], P('ply', 'gx', 'gy')
- damage: float32 [2, 24, 24, 128], P('ply', 'gx', 'gy')
Inputs may be any that keep to these rules, and one draw needn't show every extreme that they name: `counts`: blocks whose count is 0 form the plate's hole, the same through the thickness. pair_mask[a, k] equals pair_mask[a + o_k, 25 - k], o_k being the k-th offset, wherever both blocks lie in the grid.
All inputs are finite; a program needn't handle non-finite values.
Results may differ from a plain program's by a relative error of at most 0.0003.
Values sent between devices are 32-bit elements; how exact they have to be, the bound alone decides.
A program may use at most 64 MiB of HBM per device.

v0:
```python
import jax
import jax.numpy as jnp
from jax import lax
from jax.sharding import PartitionSpec as P


def padded_2(block, sides, width):
    for axis, dim in sides:
        count = lax.axis_size(axis)
        forward = [(i, i + 1) for i in range(count - 1)]
        backward = [(target, source) for source, target in forward]
        low = lax.ppermute(
            lax.slice_in_dim(block, block.shape[dim] - width, None, axis=dim), axis, forward
        )
        high = lax.ppermute(lax.slice_in_dim(block, 0, width, axis=dim), axis, backward)
        block = jnp.concatenate([low, block, high], axis=dim)
    return block


def make_offsets():
    listed = []
    for first in (-1, 0, 1):
        for second in (-1, 0, 1):
            for third in (-1, 0, 1):
                listed.append((first, second, third))
    return listed


def bell_weights(center, beside, offset):
    squared = jnp.zeros((center.shape[1], center.shape[2], center.shape[2]), jnp.float32)
    for comp in range(3):
        gap = offset[comp] + beside[comp][:, None, :] - center[comp][:, :, None]
        squared = squared + gap * gap
    return jnp.square(jnp.maximum(0.0, 1.0 - squared))


def on_device(coords, strain, kappa_old, counts, pair_mask):
    every_offset = make_offsets()
    layer_count, strip_count, block_count, point_count = strain.shape
    slots = lax.broadcasted_iota(jnp.int32, strain.shape, 3)
    active = (slots < counts[..., None]).astype(jnp.float32)
    payload = jnp.concatenate([coords, (strain * active)[None], active[None]], 0)

    def locate(padded, row_at):
        zero = row_at * 0
        layer_at = row_at // strip_count
        strip_at = row_at % strip_count
        window = lax.dynamic_slice(
            padded, (zero, layer_at, strip_at, zero, zero), (5, 3, 3, block_count + 2, point_count)
        )
        pair_flags = lax.dynamic_slice(
            pair_mask, (layer_at, strip_at, zero, zero), (1, 1, block_count, 26)
        )[0, 0].astype(jnp.float32)
        return (zero, layer_at, strip_at, window, pair_flags)

    def neighbour(window, offset):
        return window[:, 1 + offset[0], 1 + offset[1], 1 + offset[2] : 1 + offset[2] + block_count]

    rows_all = jnp.arange(layer_count * strip_count, dtype=jnp.int32)
    padded = padded_2(payload, (("ply", 1), ("gx", 2), ("gy", 3)), 1)

    def one_row(row_at):
        zero, layer_at, strip_at, window, pair_flags = locate(padded, row_at)
        center = window[:, 1, 1, 1 : block_count + 1]
        totals = jnp.zeros((2, block_count, point_count), jnp.float32)
        for which, offset in enumerate(every_offset):
            beside = neighbour(window, offset)
            weights = bell_weights(center, beside, offset)
            term = jnp.einsum("bij,cbj->cbi", weights, beside[3:5], precision=lax.Precision.HIGHEST)
            if offset != (0, 0, 0):
                flag_at = which if which < 13 else which - 1
                term = term * pair_flags[:, flag_at][None, :, None]
            totals = totals + term
        return totals

    totals = lax.map(one_row, rows_all)
    totals = totals.reshape(layer_count, strip_count, 2, block_count, point_count).transpose(
        2, 0, 1, 3, 4
    )
    weighted, weight_sum = (totals[0], totals[1])
    averaged = active * weighted / (weight_sum + 1.0 - active)
    highest = lax.pmax(jnp.max(averaged), ("ply", "gx", "gy")) + 1e-06
    kappa_new = jnp.maximum(kappa_old, 4.0 * averaged / highest)
    damage = active * (1.0 - jnp.exp(-(kappa_new - 1.0) / 2.5) / kappa_new)
    return (kappa_new, damage)


def solution(mesh):
    placed = (
        P(None, "ply", "gx", "gy", None),
        P("ply", "gx", "gy", None),
        P("ply", "gx", "gy", None),
        P("ply", "gx", "gy"),
        P("ply", "gx", "gy", None),
    )
    return jax.shard_map(
        on_device,
        mesh=mesh,
        in_specs=placed,
        out_specs=(P("ply", "gx", "gy", None), P("ply", "gx", "gy", None)),
        check_vma=False,
    )
```

profile of v0, /device:TPU:0, one launch (start us, length us, event | category | flops | bytes accessed | tf_op | source)
XLA Modules:
  0.0 253.5 jit_solution(18386238661800686719)
XLA Ops:
  2.4 4.9 %collective-permute-start = (f32[5,1,6,6,128]{4,0,3,2,1:T(8,128)S(1)}, f32[5,1,6,6,128]{4,0,3,2,1:T(8,128)S(1)}, u32[]{:S(2)}, u32[]{:S(2)}) collective-permute-start(f32[5,1,6,6,128]{4,0,3,2,1:T(8,128)S(1)} %pad_maximum_fusion.1), channel_id=1, source_target_pairs={{0,16},{1,17},{2,18},{3,19},{4,20},{5,21},{6,22},{7,23},{8,24},{9,... | collective-permute-start | bytes 276488 | tf_op jit(solution)/shard_map/ppermute | solution.py:12
  7.2 1.3 collective-permute-start.1
  8.5 1.8 collective-permute-done
  10.3 4.1 %collective-permute-done.1 = f32[5,1,6,6,128]{4,0,3,2,1:T(8,128)S(1)} collective-permute-done((f32[5,1,6,6,128]{4,0,3,2,1:T(8,128)S(1)}, f32[5,1,6,6,128]{4,0,3,2,1:T(8,128)S(1)}, u32[]{:S(2)}, u32[]{:S(2)}) %collective-permute-start.1) | collective-permute-done | bytes 92192 | tf_op jit(solution)/shard_map/ppermute | solution.py:15
  14.5 1.3 collective-permute-start.2
  15.8 1.3 collective-permute-start.3
  17.1 3.6 %collective-permute-done.3 = f32[5,3,1,6,128]{4,0,3,2,1:T(8,128)S(1)} collective-permute-done((f32[5,3,1,6,128]{4,0,3,2,1:T(8,128)S(1)}, f32[5,3,1,6,128]{4,0,3,2,1:T(8,128)S(1)}, u32[]{:S(2)}, u32[]{:S(2)}) %collective-permute-start.3) | collective-permute-done | bytes 46112 | tf_op jit(solution)/shard_map/ppermute | solution.py:15
  20.7 3.5 %collective-permute-start.4 = (f32[5,3,8,1,128]{4,0,3,2,1:T(8,128)S(1)}, f32[5,3,8,1,128]{4,0,3,2,1:T(8,128)S(1)}, u32[]{:S(2)}, u32[]{:S(2)}) collective-permute-start(f32[5,3,8,1,128]{4,0,3,2,1:T(8,128)S(1)} %get-tuple-element.275), channel_id=1, source_target_pairs={{0,1},{1,2},{2,3},{4,5},{5,6},{6,7},{8,9},{9,10},{10,11},{12,13},{... | collective-permute-start | bytes 184328 | tf_op jit(solution)/shard_map/ppermute | solution.py:12
  24.2 1.3 collective-permute-start.5
  26.4 4.3 %collective-permute-done.5 = f32[5,3,8,1,128]{4,0,3,2,1:T(8,128)S(1)} collective-permute-done((f32[5,3,8,1,128]{4,0,3,2,1:T(8,128)S(1)}, f32[5,3,8,1,128]{4,0,3,2,1:T(8,128)S(1)}, u32[]{:S(2)}, u32[]{:S(2)}) %collective-permute-start.5) | collective-permute-done | bytes 61472 | tf_op jit(solution)/shard_map/ppermute | solution.py:15
  30.9 179.9 %while.12 = (s32[]{:T(128)}, f32[6,2,6,128]{3,1,2,0:T(2,128)S(1)}, s32[6]{0:T(128)S(1)}, f32[5,3,8,8,128]{4,0,3,2,1:T(8,128)S(1)}, s32[1,6,6,26]{3,0,2,1:T(1,128...) while((s32[]{:T(128)}, f32[6,2,6,128]{3,1,2,0:T(2,128)S(1)}, ...), condition=%wide.region_1.2_spmd, body=%wide.region_0.1_spmd.sunk | while | flops 93018800 | bytes 2169382 | solution.py:76
  45.7 1.0 fusion.854
  59.8 1.0 fusion.855
  75.7 1.0 fusion.854
  89.8 1.0 fusion.855
  105.7 1.0 fusion.854
  119.8 1.0 fusion.855
  135.7 1.0 fusion.854
  149.8 1.0 fusion.855
  165.6 1.0 fusion.854
  179.8 1.0 fusion.855
  195.6 1.0 fusion.854
  209.8 1.0 fusion.855
  211.5 40.6 %pmax.7 = f32[]{:T(128)} all-reduce(f32[]{:T(128)} %get-tuple-element.86), channel_id=1, replica_groups=mesh['ply'=2,'gx'=4,'gy'=4] {'ply','gx','gy'}, use_global_device_ids=true, to_apply=%region_3.4 | all-reduce | flops 1 | bytes 8 | tf_op jit(solution)/shard_map/pmax | solution.py:82
  (456 shorter events, 167.1 us)
Async XLA Ops:
  0.6 1.7 copy-start
  2.4 7.9 %collective-permute-start = (f32[5,1,6,6,128]{4,0,3,2,1:T(8,128)S(1)}, f32[5,1,6,6,128]{4,0,3,2,1:T(8,128)S(1)}, u32[]{:S(2)}, u32[]{:S(2)}) collective-permute-start(f32[5,1,6,6,128]{4,0,3,2,1:T(8,128)S(1)} %pad_maximum_fusion.1), channel_id=1, source_target_pairs={{0,16},{1,17},{2,18},{3,19},{4,20},{5,21},{6,22},{7,23},{8,24},{9,... | collective-permute-start | bytes 276488 | tf_op jit(solution)/shard_map/ppermute | solution.py:12
  7.2 7.2 %collective-permute-start.1 = (f32[5,1,6,6,128]{4,0,3,2,1:T(8,128)S(1)}, f32[5,1,6,6,128]{4,0,3,2,1:T(8,128)S(1)}, u32[]{:S(2)}, u32[]{:S(2)}) collective-permute-start(f32[5,1,6,6,128]{4,0,3,2,1:T(8,128)S(1)} %pad_maximum_fusion.1), channel_id=1, source_target_pairs={{16,0},{17,1},{18,2},{19,3},{20,4},{21,5},{22,6},{23,7},{24,8},{25... | collective-permute-start | bytes 276488 | tf_op jit(solution)/shard_map/ppermute | solution.py:15
  14.5 2.6 %collective-permute-start.2 = (f32[5,3,1,6,128]{4,0,3,2,1:T(8,128)S(1)}, f32[5,3,1,6,128]{4,0,3,2,1:T(8,128)S(1)}, u32[]{:S(2)}, u32[]{:S(2)}) collective-permute-start(f32[5,3,1,6,128]{4,0,3,2,1:T(8,128)S(1)} %get-tuple-element.277), channel_id=1, source_target_pairs={{0,4},{4,8},{8,12},{1,5},{5,9},{9,13},{2,6},{6,10},{10,14},{3,7},{... | collective-permute-start | bytes 138248 | tf_op jit(solution)/shard_map/ppermute | solution.py:12
  15.8 4.9 %collective-permute-start.3 = (f32[5,3,1,6,128]{4,0,3,2,1:T(8,128)S(1)}, f32[5,3,1,6,128]{4,0,3,2,1:T(8,128)S(1)}, u32[]{:S(2)}, u32[]{:S(2)}) collective-permute-start(f32[5,3,1,6,128]{4,0,3,2,1:T(8,128)S(1)} %get-tuple-element.278), channel_id=1, source_target_pairs={{4,0},{8,4},{12,8},{5,1},{9,5},{13,9},{6,2},{10,6},{14,10},{7,3},{... | collective-permute-start | bytes 138248 | tf_op jit(solution)/shard_map/ppermute | solution.py:15
  20.7 5.7 %collective-permute-start.4 = (f32[5,3,8,1,128]{4,0,3,2,1:T(8,128)S(1)}, f32[5,3,8,1,128]{4,0,3,2,1:T(8,128)S(1)}, u32[]{:S(2)}, u32[]{:S(2)}) collective-permute-start(f32[5,3,8,1,128]{4,0,3,2,1:T(8,128)S(1)} %get-tuple-element.275), channel_id=1, source_target_pairs={{0,1},{1,2},{2,3},{4,5},{5,6},{6,7},{8,9},{9,10},{10,11},{12,13},{... | collective-permute-start | bytes 184328 | tf_op jit(solution)/shard_map/ppermute | solution.py:12
  24.2 6.5 %collective-permute-start.5 = (f32[5,3,8,1,128]{4,0,3,2,1:T(8,128)S(1)}, f32[5,3,8,1,128]{4,0,3,2,1:T(8,128)S(1)}, u32[]{:S(2)}, u32[]{:S(2)}) collective-permute-start(f32[5,3,8,1,128]{4,0,3,2,1:T(8,128)S(1)} %get-tuple-element.276), channel_id=1, source_target_pairs={{1,0},{2,1},{3,2},{5,4},{6,5},{7,6},{9,8},{10,9},{11,10},{13,12},{... | collective-permute-start | bytes 184328 | tf_op jit(solution)/shard_map/ppermute | solution.py:15
  210.8 41.9 %copy-start.1 = (f32[1,6,6,128]{3,0,2,1:T(1,128)S(1)}, f32[1,6,6,128]{3,0,2,1:T(1,128)}, u32[]{:S(2)}) copy-start(f32[1,6,6,128]{3,0,2,1:T(1,128)} %param.9) | copy-start | bytes 55300
where the time goes:
time: 254 us; the launch traced here: 253 us
  matrix products  163 us (64%)
  blocking collectives  40.6 us (16%)
  waiting for transfers between devices  14.7 us (6%)
  starting transfers between devices  13.5 us (5%)
  local copies, waits for them, and re-layouts  9.74 us (4%)
  other arithmetic  6.04 us (2%)
  loops' own time  4.77 us (2%)
    dot_general x162, matrix products, one_row(): jnp.einsum('bij,cbj->cbi', weights, beside[3:5], precision=lax.Precision....  163 us
    pmax x1, blocking collectives, on_device(): highest = lax.pmax(jnp.max(averaged), ('ply', 'gx', 'gy')) + 1e-06  40.6 us
    ppermute x3, waiting for transfers between devices, padded_2(): lax.ppermute(lax.slice_in_dim(block, 0, width, axis=dim), axis, backward)  12 us
    ppermute x3, starting transfers between devices, padded_2(): lax.ppermute(lax.slice_in_dim(block, block.shape[dim] - width, None, axis...  9.63 us
  transfers between devices with their start and end apart: 6, of which 5 were waited for; matrix products, arithmetic and copies ran while one was open for 0% of the time, Pallas kernels for 0%

commit v1 on v0

v1 whole, which is shorter than its diff:
```python
import functools

import jax
import jax.numpy as jnp
from jax import lax
from jax.experimental import pallas as pl
from jax.experimental.pallas import tpu as pltpu
from jax.sharding import PartitionSpec as P

MESH = pl.DeviceIdType.MESH
AXES = ("ply", "gx", "gy")
FAR = -1e30
ROWS = 32
FULL_VMEM = 48 * 1024 * 1024


def directions():
    listed = []
    for layer in (0, 1):
        for dx in (-1, 0, 1):
            for dy in (-1, 0, 1):
                if (layer, dx, dy) != (0, 0, 0):
                    listed.append((layer, dx, dy))
    return listed


def send_span(step, size):
    return {-1: (1, 1), 0: (1, size), 1: (size, 1)}[step]


def land_span(step, size):
    return {-1: (0, 1), 0: (1, size), 1: (size + 1, 1)}[step]


def halo_kernel(sizes, counts_ref, coords_ref, strain_ref, out_ref, send_sem, recv_sem):
    across, along = strain_ref.shape[1], strain_ref.shape[2]
    ply, gx, gy = (lax.axis_index(axis) for axis in AXES)
    listed = directions()

    def exists(dx, dy):
        x, y = gx + dx, gy + dy
        return (x >= 0) & (x < sizes[1]) & (y >= 0) & (y < sizes[2])

    def peer(layer, dx, dy):
        return (1 - ply if layer else ply, gx + dx, gy + dy)

    barrier = pltpu.get_barrier_semaphore()
    for layer, dx, dy in listed:
        @pl.when(exists(dx, dy))
        def _():
            pl.semaphore_signal(barrier, inc=1, device_id=peer(layer, dx, dy), device_id_type=MESH)

    slots = lax.broadcasted_iota(jnp.int32, (1, strain_ref.shape[3]), 1)
    for x in range(across):
        for y in range(along):
            for comp in range(3):
                out_ref[0, x + 1, y + 1, pl.ds(comp, 1), :] = coords_ref[comp, 0, x, pl.ds(y, 1), :]
            live = slots < counts_ref[0, x, y]
            out_ref[0, x + 1, y + 1, pl.ds(3, 1), :] = jnp.where(live, strain_ref[0, x, pl.ds(y, 1), :], 0.0)

    wide = 1 + (gx > 0).astype(jnp.int32) + (gx < sizes[1] - 1).astype(jnp.int32)
    deep = 1 + (gy > 0).astype(jnp.int32) + (gy < sizes[2] - 1).astype(jnp.int32)
    pl.semaphore_wait(barrier, 2 * wide * deep - 1)

    def sending(which):
        layer, dx, dy = listed[which]
        (x0, nx), (y0, ny) = send_span(dx, across), send_span(dy, along)
        (u0, _), (v0, _) = land_span(-dx, across), land_span(-dy, along)
        return pltpu.make_async_remote_copy(
            src_ref=out_ref.at[0, pl.ds(x0, nx), pl.ds(y0, ny)],
            dst_ref=out_ref.at[layer, pl.ds(u0, nx), pl.ds(v0, ny)],
            send_sem=send_sem.at[which],
            recv_sem=recv_sem.at[which],
            device_id=peer(layer, dx, dy),
            device_id_type=MESH,
        )

    order = sorted(range(len(listed)), key=lambda which: (listed[which][1:] != (0, 0), -listed[which][0]))
    for which in order:
        @pl.when(exists(*listed[which][1:]))
        def _():
            sending(which).start()

    for which in order:
        layer, dx, dy = listed[which]

        @pl.when(exists(dx, dy))
        def _():
            (u0, nx), (v0, ny) = land_span(dx, across), land_span(dy, along)
            (x0, _), (y0, _) = send_span(dx, across), send_span(dy, along)
            arriving = pltpu.make_async_remote_copy(
                src_ref=out_ref.at[0, pl.ds(x0, nx), pl.ds(y0, ny)],
                dst_ref=out_ref.at[layer, pl.ds(u0, nx), pl.ds(v0, ny)],
                send_sem=send_sem.at[which],
                recv_sem=recv_sem.at[listed.index((layer, -dx, -dy))],
                device_id=peer(layer, dx, dy),
                device_id_type=MESH,
            )
            arriving.wait_recv()
            sending(which).wait_send()


def average_kernel(across, along, lists_ref, counts_ref, side_ref, pack_ref, out_ref, source, column, total_w, total_s):
    points = out_ref.shape[3]
    wide, deep = across + 2, along + 2
    listed = lists_ref.shape[0] // (across * along)
    side = side_ref[0].astype(jnp.float32)
    down = lax.broadcasted_iota(jnp.int32, (deep, points), 0).astype(jnp.float32)

    for layer in range(2):
        for x in range(wide):
            at = (layer * wide + x) * deep
            place = (layer * side - 0.5, x - 0.5 * wide, down - 0.5 * deep)
            squared = jnp.zeros((deep, points), jnp.float32)
            for comp in range(3):
                spot = pack_ref[layer, x, :, comp, :] + place[comp]
                source[comp, pl.ds(at, deep), :] = spot
                squared = squared + spot * spot
            strain = pack_ref[layer, x, :, 3, :]
            source[3, pl.ds(at, deep), :] = jnp.where(strain > 0.0, -squared, FAR)
            source[4, pl.ds(at, deep), :] = strain
    for comp in range(5):
        fill = FAR if comp == 3 else 0.0
        source[comp, pl.ds(2 * wide * deep, 8), :] = jnp.full((8, points), fill, jnp.float32)

    for x in range(across):
        for y in range(along):
            at = (x + 1) * deep + y + 1
            spots = [2.0 * source[comp, pl.ds(at, 1), :] for comp in range(3)]
            rows = spots + [1.0 + source[3, pl.ds(at, 1), :], jnp.zeros((4, points), jnp.float32)]
            column[x * along + y] = jnp.concatenate(rows, 0).T

    def one_target(target, carry):
        base = target * listed
        pairs = lists_ref[base + listed - 1]

        def one_group(group, carry):
            at = pl.multiple_of(group * ROWS, ROWS)
            held = column[target, pl.ds(at, ROWS), :]
            spot = [jnp.broadcast_to(held[:, c : c + 1], (ROWS, points)) for c in range(4)]

            def one_pair(pair, sums):
                sum_w, sum_s = sums
                for half in range(2):
                    index = lists_ref[base + 2 * pair + half]
                    row = [source[c, pl.ds(index, 1), :] for c in range(5)]
                    inside = spot[0] * row[0] + spot[1] * row[1] + (spot[2] * row[2] + (spot[3] + row[3]))
                    inside = jnp.maximum(inside, 0.0)
                    weight = inside * inside
                    sum_w = sum_w + weight
                    sum_s = sum_s + weight * row[4]
                return sum_w, sum_s

            zero = jnp.zeros((ROWS, points), jnp.float32)
            sum_w, sum_s = lax.fori_loop(0, pairs, one_pair, (zero, zero))
            total_w[target, pl.ds(at, ROWS), :] = sum_w
            total_s[target, pl.ds(at, ROWS), :] = sum_s
            return carry

        return lax.fori_loop(0, (counts_ref[target] + ROWS - 1) // ROWS, one_group, carry)

    lax.fori_loop(0, across * along, one_target, 0)

    ones = jnp.ones((8, 2 * points), jnp.bfloat16)
    slots = lax.broadcasted_iota(jnp.int32, (1, points), 1)

    def lane_sums(block):
        high = block.astype(jnp.bfloat16)
        low = (block - high.astype(jnp.float32)).astype(jnp.bfloat16)
        both = jnp.concatenate([high, low], axis=1)
        summed = lax.dot_general(ones, both, (((1,), (1,)), ((), ())), preferred_element_type=jnp.float32)
        return summed[0:1]

    def finish(x, carry):
        for y in range(along):
            target = x * along + y
            weight_sum = lane_sums(total_w[target])
            weighted = lane_sums(total_s[target])
            live = slots < counts_ref[target]
            out_ref[0, x, pl.ds(y, 1), :] = jnp.where(live, weighted / jnp.where(live, weight_sum, 1.0), 0.0)
        return carry

    lax.fori_loop(0, across, finish, 0)


def highest_kernel(sizes, averaged_ref, out_ref, held, send_sem, recv_sem):
    ply, gx, gy = (lax.axis_index(axis) for axis in AXES)
    mine = ply * sizes[1] + gx
    first = sizes[0] * sizes[1]
    rounds = (
        [(1 + k, lax.rem(mine + 1 + k, first)) for k in range(first - 1)],
        [(1 + k, lax.rem(gy + 1 + k, sizes[2])) for k in range(sizes[2] - 1)],
    )

    def peer(which, index):
        return (index // sizes[1], lax.rem(index, sizes[1]), gy) if which == 0 else (ply, gx, index)

    barrier = pltpu.get_barrier_semaphore()
    for which in range(2):
        for _, index in rounds[which]:
            pl.semaphore_signal(barrier, inc=1, device_id=peer(which, index), device_id_type=MESH)
    best = jnp.max(averaged_ref[0])
    pl.semaphore_wait(barrier, len(rounds[0]) + len(rounds[1]))

    at = 0
    for which in range(2):
        held[at] = jnp.full(held.shape[1:], best, jnp.float32)
        copies = []
        for step, index in rounds[which]:
            copies.append(
                pltpu.make_async_remote_copy(
                    src_ref=held.at[at],
                    dst_ref=held.at[at + step],
                    send_sem=send_sem.at[at + step],
                    recv_sem=recv_sem.at[at + step],
                    device_id=peer(which, index),
                    device_id_type=MESH,
                )
            )
        for copy in copies:
            copy.start()
        for copy in copies:
            copy.wait()
        best = held[at]
        for step, _ in rounds[which]:
            best = jnp.maximum(best, held[at + step])
        best = best if which else jnp.max(best)
        at += len(rounds[which]) + 1
    out_ref[...] = best


def source_lists(pair_mask, sizes):
    across, along = pair_mask.shape[1:3]
    ply, gx, gy = (lax.axis_index(axis) for axis in AXES)
    wide, deep = across + 2, along + 2
    mask = pair_mask[0]
    other = jnp.where(ply == 0, mask[..., 17:26], mask[..., 0:9])
    itself = jnp.ones_like(mask[..., :1])
    flags = jnp.concatenate([mask[..., 9:13], itself, mask[..., 13:17], other], -1)
    k = jnp.arange(18, dtype=jnp.int32)
    layer, dx, dy = k // 9, k // 3 % 3 - 1, k % 3 - 1
    x = jnp.arange(across, dtype=jnp.int32)[:, None, None]
    y = jnp.arange(along, dtype=jnp.int32)[None, :, None]
    px, py = gx * across + x + dx, gy * along + y + dy
    inside = (px >= 0) & (px < sizes[1] * across) & (py >= 0) & (py < sizes[2] * along)
    taken = (flags > 0) & inside
    index = (layer * wide + x + dx + 1) * deep + y + dy + 1
    spare = 2 * wide * deep
    before = jnp.sum(jnp.where((k[None, :] < k[:, None]) & taken[..., None, :], 1, 0), -1)
    number = jnp.sum(taken.astype(jnp.int32), -1, keepdims=True)
    put = taken[..., None, :] & (before[..., None, :] == k[:, None])
    entries = spare + jnp.sum(jnp.where(put, index[..., None, :] - spare, 0), -1)
    return jnp.concatenate([entries, jnp.full_like(number, spare), (number + 1) // 2], -1).reshape(-1)


def on_device(sizes, coords, strain, kappa_old, counts, pair_mask):
    layers, across, along, points = strain.shape
    assert layers == 1 and sizes[0] == 2
    wide, deep = across + 2, along + 2
    vmem = pl.BlockSpec(memory_space=pltpu.VMEM)
    smem = pl.BlockSpec(memory_space=pltpu.SMEM)
    many = len(directions())
    packed = pl.pallas_call(
        functools.partial(halo_kernel, sizes),
        out_shape=jax.ShapeDtypeStruct((2, wide, deep, 4, points), jnp.float32),
        in_specs=[smem, vmem, vmem],
        out_specs=vmem,
        scratch_shapes=[pltpu.SemaphoreType.DMA((many,)), pltpu.SemaphoreType.DMA((many,))],
        compiler_params=pltpu.CompilerParams(collective_id=0, has_side_effects=True),
    )(counts, coords, strain)

    lists = source_lists(pair_mask, sizes)
    side = (1 - 2 * lax.axis_index("ply")).astype(jnp.int32).reshape(1)
    targets = across * along
    averaged = pl.pallas_call(
        functools.partial(average_kernel, across, along),
        out_shape=jax.ShapeDtypeStruct(strain.shape, jnp.float32),
        in_specs=[smem, smem, smem, vmem],
        out_specs=vmem,
        scratch_shapes=[
            pltpu.VMEM((5, 2 * wide * deep + 8, points), jnp.float32),
            pltpu.VMEM((targets, points, 8), jnp.float32),
            pltpu.VMEM((targets, points, points), jnp.float32),
            pltpu.VMEM((targets, points, points), jnp.float32),
        ],
        compiler_params=pltpu.CompilerParams(vmem_limit_bytes=FULL_VMEM),
    )(lists, counts.reshape(-1), side, packed)

    slots = sizes[0] * sizes[1] + sizes[2]
    highest = pl.pallas_call(
        functools.partial(highest_kernel, sizes),
        out_shape=jax.ShapeDtypeStruct((8, points), jnp.float32),
        in_specs=[vmem],
        out_specs=vmem,
        scratch_shapes=[
            pltpu.VMEM((slots, 8, points), jnp.float32),
            pltpu.SemaphoreType.DMA((slots,)),
            pltpu.SemaphoreType.DMA((slots,)),
        ],
        compiler_params=pltpu.CompilerParams(collective_id=1, has_side_effects=True),
    )(averaged)
    highest = highest[0:1, :] + 1e-06

    live = lax.broadcasted_iota(jnp.int32, strain.shape, 3) < counts[..., None]
    kappa_new = jnp.maximum(kappa_old, 4.0 * averaged / highest)
    damage = jnp.where(live, 1.0 - jnp.exp(-(kappa_new - 1.0) / 2.5) / kappa_new, 0.0)
    return (kappa_new, damage)


def solution(mesh):
    placed = (
        P(None, "ply", "gx", "gy", None),
        P("ply", "gx", "gy", None),
        P("ply", "gx", "gy", None),
        P("ply", "gx", "gy"),
        P("ply", "gx", "gy", None),
    )
    sizes = tuple(mesh.shape[axis] for axis in AXES)
    return jax.shard_map(
        functools.partial(on_device, sizes),
        mesh=mesh,
        in_specs=placed,
        out_specs=(P("ply", "gx", "gy", None), P("ply", "gx", "gy", None)),
        check_vma=False,
    )
```

time: 254 us -> 60.6 us (0.24)
  matrix products: 163 us -> 0 us
  Pallas kernels: 0 us -> 50.7 us
  blocking collectives: 40.6 us -> 0 us
  waiting for transfers between devices: 14.7 us -> 0 us
  starting transfers between devices: 13.5 us -> 0 us
  loops' own time: 4.77 us -> 0 us
  local copies, waits for them, and re-layouts: 9.74 us -> 6.47 us
  other arithmetic: 6.04 us -> 3.48 us
    dot_general x162 -> x0, matrix products: 163 us -> none  [one_row(): jnp.einsum('bij,cbj->cbi', weights, beside[3:5], precision=lax.Precision....]
    pallas_call x0 -> x3, Pallas kernels: none -> 50.7 us  [the longest x1 27.1 us: on_device(): pl.pallas_call(functools.partial(average_kernel, across, along), out_shap...]
    pmax x1 -> x0, blocking collectives: 40.6 us -> none  [on_device(): highest = lax.pmax(jnp.max(averaged), ('ply', 'gx', 'gy')) + 1e-06]
    ppermute x6 -> x0, waiting for transfers between devices: 14.7 us -> none  [the longest x3 12 us: padded_2(): lax.ppermute(lax.slice_in_dim(block, 0, width, axis=dim), axis, backward)]
    ppermute x6 -> x0, starting transfers between devices: 13.5 us -> none  [the longest x3 9.63 us: padded_2(): lax.ppermute(lax.slice_in_dim(block, block.shape[dim] - width, None, axis...]
    dynamic_slice x18 -> x0, local copies, waits for them, and re-layouts: 8.27 us -> none  [the longest x12 4.75 us: locate(): lax.dynamic_slice(pair_mask, (layer_at, strip_at, zero, zero), (1, 1, blo...]
    unnamed x6 -> x22, local copies, waits for them, and re-layouts: 0.73 us -> 6.02 us
    another operation x1 -> x0, loops' own time: 4.77 us -> none  [on_device(): totals = lax.map(one_row, rows_all)]
  transfers between devices with their start and end apart: 6 -> 0, of which waited for: 5 -> 0; matrix products, arithmetic and copies ran while one was open for 0% -> 0% of each run, Pallas kernels for 0% -> 0%
where the time goes in v1:
time: 60.6 us; the launch traced here: 61.4 us
  Pallas kernels  50.7 us (84%)
  local copies, waits for them, and re-layouts  6.47 us (11%)
  other arithmetic  3.48 us (6%)
  between operations  0.79 us (1%)
    pallas_call x1, Pallas kernels, on_device(): pl.pallas_call(functools.partial(average_kernel, across, along), out_shap...  27.1 us
    pallas_call x1, Pallas kernels, on_device(): pl.pallas_call(functools.partial(highest_kernel, sizes), out_shape=jax.Sh...  13.4 us
    pallas_call x1, Pallas kernels, on_device(): pl.pallas_call(functools.partial(halo_kernel, sizes), out_shape=jax.Shape...  10.2 us
    unnamed x22, local copies, waits for them, and re-layouts  6.02 us

profile of v1, /device:TPU:0, one launch (start us, length us, event | category | flops | bytes accessed | tf_op | source)
XLA Modules:
  0.0 61.4 jit_solution(18138894130981111659)
XLA Ops:
  0.7 0.1 add_compare_fusion.2
  0.8 0.6 copy-done.4
  1.4 0.1 slice_select_fusion
  1.5 0.3 convert_reduce_fusion
  1.8 0.7 %select_reduce_fusion.1 = s32[6,6,18]{2,1,0:T(8,128)S(1)} fusion(pred[18,18]{1,0:T(8,128)(4,1)S(1)} %iota_compare_fusion.2, pred[6,6,18]{2,1,0:T(8,128)(4,1)S(1)} %get-tuple-element.9), kind=kLoop, calls=%fused_computation.2 | loop fusion | flops 34344 | bytes 3564 | tf_op jit(solution)/shard_map/reduce_sum | solution.py:249
  2.5 0.7 %select_reduce_fusion = s32[6,6,18]{2,1,0:T(8,128)S(1)} fusion(s32[6,6,18]{2,1,0:T(8,128)S(1)} %add_add_fusion, s32[6,6,18]{2,1,0:T(8,128)S(1)} %select_reduce_fusion.1, pred[6,6,18]{2,1,0:T(8,128)(4,1)S(1)} %get-tuple-element.9), kind=kLoop, calls=%fused_computation | loop fusion | flops 46008 | bytes 8424 | tf_op jit(solution)/shard_map/reduce_sum | solution.py:252
  3.2 0.1 copy.15
  3.5 0.1 pad_add_fusion
  3.5 0.1 reshape.328.lists_ref
  3.7 0.7 %copy-done.7 = s32[1,6,6]{2,0,1:T(1,128)S(1)} copy-done((s32[1,6,6]{2,0,1:T(1,128)S(1)}, s32[1,6,6]{2,0,1:T(1,128)}, u32[]{:S(2)}) %copy-start.7) | copy-done | bytes 168
  4.3 0.6 copy.33.counts_ref
  4.9 0.6 %copy.20.coords_ref = f32[3,1,6,6,128]{4,3,2,1,0:T(8,128)} copy(f32[3,1,6,6,128]{4,1,3,2,0:T(1,128)S(1)} %copy-done.2) | data formatting | bytes 110592 | tf_op args[0]
  5.6 0.1 copy-done.5
  5.7 0.6 copy.21.strain_ref
  6.3 10.2 %shard_map.68.pack_ref = f32[2,8,8,4,128]{4,3,2,1,0:T(4,128)} custom-call(s32[1,6,6]{2,1,0:T(8,128)} %copy.33.counts_ref, f32[3,1,6,6,128]{4,3,2,1,0:T(8,128)} %copy.20.coords_ref, f32[1,6,6,128]{3,2,1,0:T(8,128)} %copy.21.strain_ref), custom_call_target="tpu_custom_call" | custom-call | tf_op jit(solution)/shard_map/pallas_call | solution.py:263
  16.5 0.1 reshape.329.counts_ref
  16.6 1.0 %copy-done = f32[2,8,8,4,128]{4,3,2,1,0:T(4,128)S(1)} copy-done((f32[2,8,8,4,128]{4,3,2,1,0:T(4,128)S(1)}, f32[2,8,8,4,128]{4,3,2,1,0:T(4,128)}, u32[]{:S(2)}) %copy-start) | copy-done | bytes 262168
  17.5 27.1 %shard_map.69.averaged_ref = f32[1,6,6,128]{3,2,1,0:T(8,128)S(1)} custom-call(s32[720]{0:T(1024)S(1)} %reshape.328.lists_ref, s32[36]{0:T(128)S(1)} %reshape.329.counts_ref, s32[1]{0:T(128)} %bitcast.1.side_ref, f32[2,8,8,4,128]{4,3,2,1,0:T(4,128)S(1)} %copy-done), custom_call_target="tpu_custom_call" | custom-call | tf_op jit(solution)/shard_map/pallas_call | solution.py:275
  44.7 0.6 %copy-done.1 = f32[1,6,6,128]{3,2,1,0:T(8,128)} copy-done((f32[1,6,6,128]{3,2,1,0:T(8,128)}, f32[1,6,6,128]{3,2,1,0:T(8,128)S(1)}, u32[]{:S(2)}) %copy-start.1) | copy-done | bytes 18456
  45.3 13.4 %shard_map.70 = f32[8,128]{1,0:T(8,128)} custom-call(f32[1,6,6,128]{3,2,1,0:T(8,128)} %copy-done.1), custom_call_target="tpu_custom_call" | custom-call | tf_op jit(solution)/shard_map/pallas_call | solution.py:290
  58.7 0.7 %add_bitcast_fusion.1 = f32[128]{0:T(128)S(1)} fusion(f32[8,128]{1,0:T(8,128)} %shard_map.70), kind=kLoop, calls=%fused_computation.43 | loop fusion | flops 128 | bytes 1024 | tf_op jit(solution)/shard_map/div | solution.py:305
  59.4 0.8 %subtract_select_fusion = (f32[1,6,6,128]{3,2,1,0:T(8,128)S(1)}, f32[1,6,6,128]{3,2,1,0:T(8,128)S(1)}) fusion(s32[6,6]{1,0:T(8,128)S(1)} %bitcast.13, f32[128]{0:T(128)S(1)} %add_bitcast_fusion.1, f32[1,6,6,128]{3,2,1,0:T(8,128)} %copy-done.1, f32[1,6,6,128]{3,0,2,1:T(1,128)S(1)} %copy-done.6), kind=kLoop, calls=%fused_computation.14 | loop fusion | flops 46080 | bytes 74384 | tf_op jit(solution)/shard_map/jit(_where)/select_n | solution.py:306
  60.2 0.6 %copy.23 = f32[1,6,6,128]{3,0,2,1:T(1,128)} copy(f32[1,6,6,128]{3,2,1,0:T(8,128)S(1)} %get-tuple-element.7) | data formatting | bytes 36864
  60.8 0.6 %copy.24 = f32[1,6,6,128]{3,0,2,1:T(1,128)} copy(f32[1,6,6,128]{3,2,1,0:T(8,128)S(1)} %get-tuple-element.6) | data formatting | bytes 36864
  (27 shorter events, 0.3 us)
Async XLA Ops:
  0.6 0.7 %copy-start.4 = (s32[1,6,6,26]{3,0,2,1:T(1,128)S(1)}, s32[1,6,6,26]{3,0,2,1:T(1,128)}, u32[]{:S(2)}) copy-start(s32[1,6,6,26]{3,0,2,1:T(1,128)} %param.9) | copy-start | bytes 11236
  3.5 1.5 %copy-start.2 = (f32[3,1,6,6,128]{4,1,3,2,0:T(1,128)S(1)}, f32[3,1,6,6,128]{4,1,3,2,0:T(1,128)}, u32[]{:S(2)}) copy-start(f32[3,1,6,6,128]{4,1,3,2,0:T(1,128)} %param.5) | copy-start | bytes 165892
  3.7 0.7 %copy-start.7 = (s32[1,6,6]{2,0,1:T(1,128)S(1)}, s32[1,6,6]{2,0,1:T(1,128)}, u32[]{:S(2)}) copy-start(s32[1,6,6]{2,0,1:T(1,128)} %param.8) | copy-start | bytes 436
  4.9 0.7 %copy-start.5 = (f32[1,6,6,128]{3,0,2,1:T(1,128)S(1)}, f32[1,6,6,128]{3,0,2,1:T(1,128)}, u32[]{:S(2)}) copy-start(f32[1,6,6,128]{3,0,2,1:T(1,128)} %param.6) | copy-start | bytes 55300
  16.6 1.0 %copy-start = (f32[2,8,8,4,128]{4,3,2,1,0:T(4,128)S(1)}, f32[2,8,8,4,128]{4,3,2,1,0:T(4,128)}, u32[]{:S(2)}) copy-start(f32[2,8,8,4,128]{4,3,2,1,0:T(4,128)} %shard_map.68.pack_ref) | copy-start | bytes 786436
  44.7 0.6 %copy-start.1 = (f32[1,6,6,128]{3,2,1,0:T(8,128)}, f32[1,6,6,128]{3,2,1,0:T(8,128)S(1)}, u32[]{:S(2)}) copy-start(f32[1,6,6,128]{3,2,1,0:T(8,128)S(1)} %shard_map.69.averaged_ref) | copy-start | bytes 55300
  45.3 14.1 %copy-start.3 = (s32[1,6,6]{2,1,0:T(8,128)S(1)}, s32[1,6,6]{2,1,0:T(8,128)}, u32[]{:S(2)}) copy-start(s32[1,6,6]{2,1,0:T(8,128)} %copy.33.counts_ref) | copy-start | bytes 436
  45.3 14.1 %copy-start.6 = (f32[1,6,6,128]{3,0,2,1:T(1,128)S(1)}, f32[1,6,6,128]{3,0,2,1:T(1,128)}, u32[]{:S(2)}) copy-start(f32[1,6,6,128]{3,0,2,1:T(1,128)} %param.7) | copy-start | bytes 55300

commit v2 on v1

v2 whole, which is shorter than its diff:
```python
import functools

import jax
import jax.numpy as jnp
from jax import lax
from jax.experimental import pallas as pl
from jax.experimental.pallas import tpu as pltpu
from jax.sharding import PartitionSpec as P

MESH = pl.DeviceIdType.MESH
AXES = ("ply", "gx", "gy")
FAR = -1e30
ROWS = 32
DEPTH = 32
FULL_VMEM = 48 * 1024 * 1024


def directions():
    listed = []
    for layer in (0, 1):
        for dx in (-1, 0, 1):
            for dy in (-1, 0, 1):
                if (layer, dx, dy) != (0, 0, 0):
                    listed.append((layer, dx, dy))
    return listed


def send_span(step, size):
    return {-1: (1, 1), 0: (1, size), 1: (size, 1)}[step]


def land_span(step, size):
    return {-1: (0, 1), 0: (1, size), 1: (size + 1, 1)}[step]


def damage_kernel(sizes, counts_ref, mask_ref, coords_ref, strain_ref, kappa_ref, kappa_out, damage_out,
                  pack, source, target_side, total_w, total_s, averaged, held, send_sem, recv_sem, max_send, max_recv):
    across, along, points = strain_ref.shape[1:]
    wide, deep = across + 2, along + 2
    ply, gx, gy = (lax.axis_index(axis) for axis in AXES)
    listed = directions()

    def exists(dx, dy):
        x, y = gx + dx, gy + dy
        return (x >= 0) & (x < sizes[1]) & (y >= 0) & (y < sizes[2])

    def peer(layer, dx, dy):
        return (1 - ply if layer else ply, gx + dx, gy + dy)

    mine = ply * sizes[1] + gx
    first = sizes[0] * sizes[1]
    rounds = (
        [(1 + k, lax.rem(mine + 1 + k, first)) for k in range(first - 1)],
        [(1 + k, lax.rem(gy + 1 + k, sizes[2])) for k in range(sizes[2] - 1)],
    )

    def max_peer(which, index):
        return (index // sizes[1], lax.rem(index, sizes[1]), gy) if which == 0 else (ply, gx, index)

    pack[...] = jnp.zeros(pack.shape, jnp.float32)
    barrier = pltpu.get_barrier_semaphore()
    for layer, dx, dy in listed:
        @pl.when(exists(dx, dy))
        def _():
            pl.semaphore_signal(barrier, inc=1, device_id=peer(layer, dx, dy), device_id_type=MESH)
    for which in range(2):
        for _, index in rounds[which]:
            pl.semaphore_signal(barrier, inc=1, device_id=max_peer(which, index), device_id_type=MESH)

    slots = lax.broadcasted_iota(jnp.int32, (1, points), 1)
    for x in range(across):
        for y in range(along):
            for comp in range(3):
                pack[0, x + 1, y + 1, pl.ds(comp, 1), :] = coords_ref[comp, 0, x, pl.ds(y, 1), :]
            live = slots < counts_ref[0, x, y]
            pack[0, x + 1, y + 1, pl.ds(3, 1), :] = jnp.where(live, strain_ref[0, x, pl.ds(y, 1), :], 0.0)

    wide_peers = 1 + (gx > 0).astype(jnp.int32) + (gx < sizes[1] - 1).astype(jnp.int32)
    deep_peers = 1 + (gy > 0).astype(jnp.int32) + (gy < sizes[2] - 1).astype(jnp.int32)
    pl.semaphore_wait(barrier, 2 * wide_peers * deep_peers - 1 + len(rounds[0]) + len(rounds[1]))

    def sending(which):
        layer, dx, dy = listed[which]
        (x0, nx), (y0, ny) = send_span(dx, across), send_span(dy, along)
        (u0, _), (v0, _) = land_span(-dx, across), land_span(-dy, along)
        return pltpu.make_async_remote_copy(
            src_ref=pack.at[0, pl.ds(x0, nx), pl.ds(y0, ny)],
            dst_ref=pack.at[layer, pl.ds(u0, nx), pl.ds(v0, ny)],
            send_sem=send_sem.at[which],
            recv_sem=recv_sem.at[which],
            device_id=peer(layer, dx, dy),
            device_id_type=MESH,
        )

    order = sorted(range(len(listed)), key=lambda which: (listed[which][1:] != (0, 0), -listed[which][0]))
    for which in order:
        @pl.when(exists(*listed[which][1:]))
        def _():
            sending(which).start()

    side = (1 - 2 * ply).astype(jnp.float32)
    sub = lax.broadcasted_iota(jnp.int32, (8, points), 0)
    top = sub < 4
    row = jnp.where(top, sub, sub - 4)
    last = jnp.where(top, 1.0, 0.0)

    def split(rows):
        high = rows.astype(jnp.bfloat16).astype(jnp.float32)
        rest = rows - high
        middle = rest.astype(jnp.bfloat16).astype(jnp.float32)
        return high, middle, rest - middle

    def spots(layer, x, y):
        origin = (layer * side - 0.5, x - 0.5 * wide, y - 0.5 * deep)
        found = [
            jnp.broadcast_to(pack[layer, x, y, pl.ds(comp, 1), :], (8, points)) + origin[comp] for comp in range(3)
        ]
        return found, found[0] * found[0] + found[1] * found[1] + found[2] * found[2]

    def stack(rows):
        return jnp.where(row == 0, rows[0], jnp.where(row == 1, rows[1], jnp.where(row == 2, rows[2], rows[3])))

    def build_source(layer, x, y, found, squared):
        strain = jnp.broadcast_to(pack[layer, x, y, pl.ds(3, 1), :], (8, points))
        high, middle, low = split(stack(found + [jnp.where(strain > 0.0, -squared, FAR)]))
        pair = jnp.where(top, high, middle)
        rows = jnp.concatenate([pair, jnp.where(top, high, low), pair, last], 0)
        source[layer, x, :, pl.ds(y * points, points)] = rows.astype(jnp.bfloat16)

    def build_target(x, y, found, squared):
        high, middle, low = split(stack([2.0 * spot for spot in found] + [jnp.ones((8, points), jnp.float32)]))
        a_high, a_middle, a_low = split(1.0 - squared)
        own = jnp.where(sub == 0, a_high, jnp.where(sub == 1, a_middle, jnp.where(sub == 2, a_low, 0.0)))
        rows = jnp.concatenate([high, jnp.where(top, middle, high), jnp.where(top, low, middle), own], 0)
        target_side[(x - 1) * along + y - 1] = rows.T.astype(jnp.bfloat16)

    def own_row(x, carry):
        for y in range(1, along + 1):
            found, squared = spots(0, x, y)
            build_source(0, x, y, found, squared)
            build_target(x, y, found, squared)
        return carry

    lax.fori_loop(1, across + 1, own_row, 0)

    mask_base = jnp.where(ply == 0, 17, 0)

    def mask_of(layer, x, y, near):
        if layer:
            return mask_ref[0, x, y, mask_base + near].astype(jnp.float32)
        if near == 4:
            return None
        return mask_ref[0, x, y, 9 + near - (near > 4)].astype(jnp.float32)

    def sums_of(x, y, layer):
        beside = jnp.concatenate(
            [source[layer, x + step, :, pl.ds(y * points, 3 * points)] for step in range(3)], axis=1
        )
        inside = jnp.dot(target_side[x * along + y], beside, preferred_element_type=jnp.float32)
        flags, strains = [], []
        for near in range(9):
            strain = pack[layer, x + near // 3, y + near % 3, pl.ds(3, 1), :]
            flag = mask_of(layer, x, y, near)
            flags.append(flag)
            strains.append(strain if flag is None else strain * flag)
        parts = []
        for at in range(0, points, ROWS):
            sum_w = sum_s = None
            for near in range(9):
                weight = jnp.maximum(inside[at : at + ROWS, near * points : (near + 1) * points], 0.0)
                weight = weight * weight
                term_w = weight if flags[near] is None else weight * flags[near]
                term_s = weight * strains[near]
                sum_w = term_w if sum_w is None else sum_w + term_w
                sum_s = term_s if sum_s is None else sum_s + term_s
            parts.append((at, sum_w, sum_s))
        return parts

    def own_layer(x, ys):
        for y in ys:
            for at, sum_w, sum_s in sums_of(x, y, 0):
                total_w[x * along + y, pl.ds(at, ROWS), :] = sum_w
                total_s[x * along + y, pl.ds(at, ROWS), :] = sum_s

    def inner_row(x, carry):
        own_layer(x, range(1, along - 1))
        return carry

    lax.fori_loop(1, across - 1, inner_row, 0)

    for which in order:
        layer, dx, dy = listed[which]

        @pl.when(exists(dx, dy))
        def _():
            (u0, nx), (v0, ny) = land_span(dx, across), land_span(dy, along)
            (x0, _), (y0, _) = send_span(dx, across), send_span(dy, along)
            arriving = pltpu.make_async_remote_copy(
                src_ref=pack.at[0, pl.ds(x0, nx), pl.ds(y0, ny)],
                dst_ref=pack.at[layer, pl.ds(u0, nx), pl.ds(v0, ny)],
                send_sem=send_sem.at[which],
                recv_sem=recv_sem.at[listed.index((layer, -dx, -dy))],
                device_id=peer(layer, dx, dy),
                device_id_type=MESH,
            )
            arriving.wait_recv()
            sending(which).wait_send()

    def halo_row(x, carry):
        for y in range(deep):
            build_source(1, x, y, *spots(1, x, y))
        for y in (0, deep - 1):
            build_source(0, x, y, *spots(0, x, y))
        return carry

    def halo_end(end, carry):
        x = end * (wide - 1)
        for y in range(1, deep - 1):
            build_source(0, x, y, *spots(0, x, y))
        return carry

    lax.fori_loop(0, wide, halo_row, 0)
    lax.fori_loop(0, 2, halo_end, 0)

    def edge_row(x, carry):
        own_layer(x, (0, along - 1))
        return carry

    def end_row(end, carry):
        own_layer(end * (across - 1), range(along))
        return carry

    lax.fori_loop(1, across - 1, edge_row, 0)
    lax.fori_loop(0, 2, end_row, 0)

    ones = jnp.ones((8, 2 * points), jnp.bfloat16)

    def lane_sums(block):
        high = block.astype(jnp.bfloat16)
        low = (block - high.astype(jnp.float32)).astype(jnp.bfloat16)
        both = jnp.concatenate([high, low], axis=1)
        summed = lax.dot_general(ones, both, (((1,), (1,)), ((), ())), preferred_element_type=jnp.float32)
        return summed[0:1]

    def other_layer(x, carry):
        for y in range(along):
            target = x * along + y
            parts = sums_of(x, y, 1)
            weight_sum = lane_sums(jnp.concatenate([w + total_w[target, pl.ds(at, ROWS), :] for at, w, _ in parts], 0))
            weighted = lane_sums(jnp.concatenate([s + total_s[target, pl.ds(at, ROWS), :] for at, _, s in parts], 0))
            live = slots < counts_ref[0, x, y]
            averaged[x, pl.ds(y, 1), :] = jnp.where(live, weighted / jnp.where(live, weight_sum, 1.0), 0.0)
        return carry

    lax.fori_loop(0, across, other_layer, 0)

    best = jnp.max(averaged[...])
    at = 0
    for which in range(2):
        held[at] = jnp.full(held.shape[1:], best, jnp.float32)
        copies = []
        for step, index in rounds[which]:
            copies.append(
                pltpu.make_async_remote_copy(
                    src_ref=held.at[at],
                    dst_ref=held.at[at + step],
                    send_sem=max_send.at[at + step],
                    recv_sem=max_recv.at[at + step],
                    device_id=max_peer(which, index),
                    device_id_type=MESH,
                )
            )
        for copy in copies:
            copy.start()
        for copy in copies:
            copy.wait()
        best = held[at]
        for step, _ in rounds[which]:
            best = jnp.maximum(best, held[at + step])
        best = best if which else jnp.max(best)
        at += len(rounds[which]) + 1

    scale = 4.0 / (best[0:1] + 1e-06)
    for x in range(across):
        kappa = jnp.maximum(kappa_ref[0, x], averaged[x] * scale)
        kappa_out[0, x] = kappa
        grown = 1.0 - jnp.exp(-(kappa - 1.0) / 2.5) / kappa
        for y in range(along):
            live = slots < counts_ref[0, x, y]
            damage_out[0, x, pl.ds(y, 1), :] = jnp.where(live, grown[y : y + 1], 0.0)


def on_device(sizes, coords, strain, kappa_old, counts, pair_mask):
    layers, across, along, points = strain.shape
    assert layers == 1 and sizes[0] == 2
    wide, deep = across + 2, along + 2
    vmem = pl.BlockSpec(memory_space=pltpu.VMEM)
    smem = pl.BlockSpec(memory_space=pltpu.SMEM)
    many = len(directions())
    targets = across * along
    slots = sizes[0] * sizes[1] + sizes[2]
    return pl.pallas_call(
        functools.partial(damage_kernel, sizes),
        out_shape=(jax.ShapeDtypeStruct(strain.shape, jnp.float32), jax.ShapeDtypeStruct(strain.shape, jnp.float32)),
        in_specs=[smem, smem, vmem, vmem, vmem],
        out_specs=(vmem, vmem),
        scratch_shapes=[
            pltpu.VMEM((2, wide, deep, 4, points), jnp.float32),
            pltpu.VMEM((2, wide, DEPTH, deep * points), jnp.bfloat16),
            pltpu.VMEM((targets, points, DEPTH), jnp.bfloat16),
            pltpu.VMEM((targets, points, points), jnp.float32),
            pltpu.VMEM((targets, points, points), jnp.float32),
            pltpu.VMEM((across, along, points), jnp.float32),
            pltpu.VMEM((slots, 8, points), jnp.float32),
            pltpu.SemaphoreType.DMA((many,)),
            pltpu.SemaphoreType.DMA((many,)),
            pltpu.SemaphoreType.DMA((slots,)),
            pltpu.SemaphoreType.DMA((slots,)),
        ],
        compiler_params=pltpu.CompilerParams(collective_id=0, has_side_effects=True, vmem_limit_bytes=FULL_VMEM),
    )(counts, pair_mask, coords, strain, kappa_old)


def solution(mesh):
    placed = (
        P(None, "ply", "gx", "gy", None),
        P("ply", "gx", "gy", None),
        P("ply", "gx", "gy", None),
        P("ply", "gx", "gy"),
        P("ply", "gx", "gy", None),
    )
    sizes = tuple(mesh.shape[axis] for axis in AXES)
    return jax.shard_map(
        functools.partial(on_device, sizes),
        mesh=mesh,
        in_specs=placed,
        out_specs=(P("ply", "gx", "gy", None), P("ply", "gx", "gy", None)),
        check_vma=False,
    )
```

time: 60.6 us -> 37.6 us (0.62); the launches traced: 61.4 us -> 37.4 us
  Pallas kernels: 50.7 us -> 33.3 us
  other arithmetic: 3.48 us -> 0 us
  local copies, waits for them, and re-layouts: 6.47 us -> 3.41 us
    pallas_call x3 -> x1, Pallas kernels: 50.7 us -> 33.3 us  [on_device(): pl.pallas_call(functools.partial(damage_kernel, sizes), out_shape=(jax.Sh...]
    unnamed x22 -> x11, local copies, waits for them, and re-layouts: 6.02 us -> 2.16 us
    reduce_sum x3 -> x0, other arithmetic: 1.64 us -> none  [the longest x1 0.69 us: source_lists(): jnp.sum(jnp.where((k[None, :] < k[:, None]) & taken[..., None, :], 1, 0),...]
    pallas_call x0 -> x2, local copies, waits for them, and re-layouts: none -> 1.25 us  [on_device(): pl.pallas_call(functools.partial(damage_kernel, sizes), out_shape=(jax.Sh...]
    select_n x3 -> x0, other arithmetic: 0.91 us -> none  [the longest x1 0.81 us: on_device(): jnp.where(live, 1.0 - jnp.exp(-(kappa_new - 1.0) / 2.5) / kappa_new, 0.0)]
    div x1 -> x0, other arithmetic: 0.68 us -> none  [on_device(): kappa_new = jnp.maximum(kappa_old, 4.0 * averaged / highest)]
where the time goes in v2:
time: 37.6 us; the launch traced here: 37.4 us
  Pallas kernels  33.3 us (89%)
  local copies, waits for them, and re-layouts  3.41 us (9%)
  between operations  0.66 us (2%)
    pallas_call x1, Pallas kernels, on_device(): pl.pallas_call(functools.partial(damage_kernel, sizes), out_shape=(jax.Sh...  33.3 us
    unnamed x11, local copies, waits for them, and re-layouts  2.16 us
    pallas_call x2, local copies, waits for them, and re-layouts, on_device(): pl.pallas_call(functools.partial(damage_kernel, sizes), out_shape=(jax.Sh...  1.25 us

profile of v2, /device:TPU:0, one launch (start us, length us, event | category | flops | bytes accessed | tf_op | source)
XLA Modules:
  0.0 37.4 jit_solution(17575872865633866442)
XLA Ops:
  0.6 0.0 copy-start.1
  0.6 0.7 %copy.7.counts_ref = s32[1,6,6]{2,1,0:T(8,128)S(1)} copy(s32[1,6,6]{2,0,1:T(1,128)} %param.8) | data formatting | bytes 288 | tf_op args[3]
  1.3 0.0 copy-start
  1.3 0.7 %copy.10.strain_ref = f32[1,6,6,128]{3,2,1,0:T(8,128)S(1)} copy(f32[1,6,6,128]{3,0,2,1:T(1,128)} %param.6) | data formatting | bytes 36864 | tf_op args[1]
  2.1 0.0 copy-done.1
  2.1 0.0 copy-start.2
  2.1 0.7 %copy-done.2 = s32[1,6,6,26]{3,0,2,1:T(1,128)S(1)} copy-done((s32[1,6,6,26]{3,0,2,1:T(1,128)S(1)}, s32[1,6,6,26]{3,0,2,1:T(1,128)}, u32[]{:S(2)}) %copy-start.2) | copy-done | bytes 3768
  2.8 0.0 copy-done
  2.8 33.3 %shard_map.68 = (f32[1,6,6,128]{3,2,1,0:T(8,128)S(1)}, f32[1,6,6,128]{3,2,1,0:T(8,128)S(1)}) custom-call(s32[1,6,6]{2,1,0:T(8,128)S(1)} %copy.7.counts_ref, s32[1,6,6,26]{3,2,1,0:T(8,128)S(1)} %copy.8.mask_ref, f32[3,1,6,6,128]{4,3,2,1,0:T(8,128)S(1)} %copy.9.coords_ref, f32[1,6,6,128]{3,2,1,0:T(8,128)S(1)} %copy.10.strain_ref, ...), custom_call_target="tpu_custom_call" | custom-call | tf_op jit(solution)/shard_map/pallas_call | solution.py:302
  36.1 0.6 %copy.12 = f32[1,6,6,128]{3,0,2,1:T(1,128)} copy(f32[1,6,6,128]{3,2,1,0:T(8,128)S(1)} %get-tuple-element.2) | data formatting | bytes 36864 | tf_op jit(solution)/shard_map/pallas_call | solution.py:302
  36.7 0.6 %copy.13 = f32[1,6,6,128]{3,0,2,1:T(1,128)} copy(f32[1,6,6,128]{3,2,1,0:T(8,128)S(1)} %get-tuple-element.3) | data formatting | bytes 36864 | tf_op jit(solution)/shard_map/pallas_call | solution.py:302
  (3 shorter events, 0.0 us)
Async XLA Ops:
  0.6 1.4 %copy-start.1 = (f32[1,6,6,128]{3,0,2,1:T(1,128)S(1)}, f32[1,6,6,128]{3,0,2,1:T(1,128)}, u32[]{:S(2)}) copy-start(f32[1,6,6,128]{3,0,2,1:T(1,128)} %param.7) | copy-start | bytes 55300
  1.3 1.5 %copy-start = (f32[3,1,6,6,128]{4,1,3,2,0:T(1,128)S(1)}, f32[3,1,6,6,128]{4,1,3,2,0:T(1,128)}, u32[]{:S(2)}) copy-start(f32[3,1,6,6,128]{4,1,3,2,0:T(1,128)} %param.5) | copy-start | bytes 165892
  2.1 0.7 %copy-start.2 = (s32[1,6,6,26]{3,0,2,1:T(1,128)S(1)}, s32[1,6,6,26]{3,0,2,1:T(1,128)}, u32[]{:S(2)}) copy-start(s32[1,6,6,26]{3,0,2,1:T(1,128)} %param.9) | copy-start | bytes 11236

commit v3 on v2

--- a/solution.py
+++ b/solution.py
@@ -10,8 +10,9 @@
 MESH = pl.DeviceIdType.MESH
 AXES = ("ply", "gx", "gy")
 FAR = -1e30
-ROWS = 32
+ROWS = 64
 DEPTH = 32
+AHEAD = 2
 FULL_VMEM = 48 * 1024 * 1024
 
 
@@ -35,7 +36,7 @@
 
 def damage_kernel(sizes, counts_ref, mask_ref, coords_ref, strain_ref, kappa_ref, kappa_out, damage_out,
                   pack, source, target_side, total_w, total_s, averaged, held, send_sem, recv_sem, max_send, max_recv):
-    across, along, points = strain_ref.shape[1:]
+    across, along, _, points = strain_ref.shape
     wide, deep = across + 2, along + 2
     ply, gx, gy = (lax.axis_index(axis) for axis in AXES)
     listed = directions()
@@ -71,9 +72,9 @@
     for x in range(across):
         for y in range(along):
             for comp in range(3):
-                pack[0, x + 1, y + 1, pl.ds(comp, 1), :] = coords_ref[comp, 0, x, pl.ds(y, 1), :]
-            live = slots < counts_ref[0, x, y]
-            pack[0, x + 1, y + 1, pl.ds(3, 1), :] = jnp.where(live, strain_ref[0, x, pl.ds(y, 1), :], 0.0)
+                pack[0, x + 1, y + 1, pl.ds(comp, 1), :] = coords_ref[comp, x, y]
+            live = slots < counts_ref[x, 0, y]
+            pack[0, x + 1, y + 1, pl.ds(3, 1), :] = jnp.where(live, strain_ref[x, y], 0.0)
 
     wide_peers = 1 + (gx > 0).astype(jnp.int32) + (gx < sizes[1] - 1).astype(jnp.int32)
     deep_peers = 1 + (gy > 0).astype(jnp.int32) + (gy < sizes[2] - 1).astype(jnp.int32)
@@ -130,7 +131,7 @@
     def build_target(x, y, found, squared):
         high, middle, low = split(stack([2.0 * spot for spot in found] + [jnp.ones((8, points), jnp.float32)]))
         a_high, a_middle, a_low = split(1.0 - squared)
-        own = jnp.where(sub == 0, a_high, jnp.where(sub == 1, a_middle, jnp.where(sub == 2, a_low, 0.0)))
+        own = jnp.where(sub == 0, a_high, jnp.where(sub == 1, a_middle, jnp.where(sub == 2, a_low, jnp.where(sub == 4, 1.0, 0.0))))
         rows = jnp.concatenate([high, jnp.where(top, middle, high), jnp.where(top, low, middle), own], 0)
         target_side[(x - 1) * along + y - 1] = rows.T.astype(jnp.bfloat16)
 
@@ -145,42 +146,53 @@
 
     mask_base = jnp.where(ply == 0, 17, 0)
 
-    def mask_of(layer, x, y, near):
-        if layer:
-            return mask_ref[0, x, y, mask_base + near].astype(jnp.float32)
-        if near == 4:
-            return None
-        return mask_ref[0, x, y, 9 + near - (near > 4)].astype(jnp.float32)
-
-    def sums_of(x, y, layer):
-        beside = jnp.concatenate(
-            [source[layer, x + step, :, pl.ds(y * points, 3 * points)] for step in range(3)], axis=1
-        )
-        inside = jnp.dot(target_side[x * along + y], beside, preferred_element_type=jnp.float32)
-        flags, strains = [], []
-        for near in range(9):
-            strain = pack[layer, x + near // 3, y + near % 3, pl.ds(3, 1), :]
-            flag = mask_of(layer, x, y, near)
-            flags.append(flag)
-            strains.append(strain if flag is None else strain * flag)
-        parts = []
-        for at in range(0, points, ROWS):
-            sum_w = sum_s = None
-            for near in range(9):
-                weight = jnp.maximum(inside[at : at + ROWS, near * points : (near + 1) * points], 0.0)
+    half_rows = lax.broadcasted_iota(jnp.int32, (DEPTH // 2, points), 0)
+    mask_row = jnp.where(half_rows == 12, 1.0, 0.0).astype(jnp.bfloat16)
+
+    def masked_source(layer, x, y, near):
+        block = source[layer, x + near // 3, :, pl.ds((y + near % 3) * points, points)]
+        if layer == 0 and near == 4:
+            return block
+        flag = mask_ref[x, y, 0, mask_base + near if layer else 9 + near - (near > 4)]
+        away = jnp.full(mask_row.shape, FAR * (1 - flag).astype(jnp.float32)).astype(jnp.bfloat16)
+        return jnp.concatenate([block[: DEPTH // 2], block[DEPTH // 2 :] + mask_row * away], 0)
+
+    def row_sums(x, ys, layer):
+        tasks = [(y, at, pair) for y in ys for at in range(0, points, ROWS) for pair in range(0, 9, 2)]
+        sides = {}
+
+        def product(task):
+            y, at, pair = task
+            nears = [near for near in (pair, pair + 1) if near < 9]
+            for near in nears:
+                if (y, near) not in sides:
+                    sides[y, near] = masked_source(layer, x, y, near)
+            beside = jnp.concatenate([sides[y, near] for near in nears], axis=1)
+            rows = target_side[x * along + y, pl.ds(at, ROWS), :]
+            return nears, jnp.dot(rows, beside, preferred_element_type=jnp.float32)
+
+        ready = [product(task) for task in tasks[:AHEAD]]
+        sum_w = sum_s = None
+        for k, (y, at, pair) in enumerate(tasks):
+            if k + AHEAD < len(tasks):
+                ready.append(product(tasks[k + AHEAD]))
+            nears, inside = ready.pop(0)
+            for slot, near in enumerate(nears):
+                weight = jnp.maximum(inside[:, slot * points : (slot + 1) * points], 0.0)
                 weight = weight * weight
-                term_w = weight if flags[near] is None else weight * flags[near]
-                term_s = weight * strains[near]
-                sum_w = term_w if sum_w is None else sum_w + term_w
-                sum_s = term_s if sum_s is None else sum_s + term_s
-            parts.append((at, sum_w, sum_s))
-        return parts
+                term = weight * pack[layer, x + near // 3, y + near % 3, pl.ds(3, 1), :]
+                sum_w = weight if near == 0 else sum_w + weight
+                sum_s = term if near == 0 else sum_s + term
+            if pair == 8:
+                place = (x * along + y, pl.ds(at, ROWS))
+                if layer:
+                    sum_w = sum_w + total_w[place]
+                    sum_s = sum_s + total_s[place]
+                total_w[place] = sum_w
+                total_s[place] = sum_s
 
     def own_layer(x, ys):
-        for y in ys:
-            for at, sum_w, sum_s in sums_of(x, y, 0):
-                total_w[x * along + y, pl.ds(at, ROWS), :] = sum_w
-                total_s[x * along + y, pl.ds(at, ROWS), :] = sum_s
+        row_sums(x, ys, 0)
 
     def inner_row(x, carry):
         own_layer(x, range(1, along - 1))
@@ -233,6 +245,12 @@
     lax.fori_loop(1, across - 1, edge_row, 0)
     lax.fori_loop(0, 2, end_row, 0)
 
+    def other_layer(x, carry):
+        row_sums(x, range(along), 1)
+        return carry
+
+    lax.fori_loop(0, across, other_layer, 0)
+
     ones = jnp.ones((8, 2 * points), jnp.bfloat16)
 
     def lane_sums(block):
@@ -242,17 +260,18 @@
         summed = lax.dot_general(ones, both, (((1,), (1,)), ((), ())), preferred_element_type=jnp.float32)
         return summed[0:1]
 
-    def other_layer(x, carry):
+    def divide(x, carry):
+        these = pl.ds(x * along, along)
+        weight_sum = lane_sums(total_w[these].reshape(along * points, points))
+        weighted = lane_sums(total_s[these].reshape(along * points, points))
         for y in range(along):
-            target = x * along + y
-            parts = sums_of(x, y, 1)
-            weight_sum = lane_sums(jnp.concatenate([w + total_w[target, pl.ds(at, ROWS), :] for at, w, _ in parts], 0))
-            weighted = lane_sums(jnp.concatenate([s + total_s[target, pl.ds(at, ROWS), :] for at, _, s in parts], 0))
-            live = slots < counts_ref[0, x, y]
-            averaged[x, pl.ds(y, 1), :] = jnp.where(live, weighted / jnp.where(live, weight_sum, 1.0), 0.0)
-        return carry
-
-    lax.fori_loop(0, across, other_layer, 0)
+            span = slice(y * points, (y + 1) * points)
+            live = slots < counts_ref[x, 0, y]
+            share = weighted[:, span] / jnp.where(live, weight_sum[:, span], 1.0)
+            averaged[x, pl.ds(y, 1), :] = jnp.where(live, share, 0.0)
+        return carry
+
+    lax.fori_loop(0, across, divide, 0)
 
     best = jnp.max(averaged[...])
     at = 0
@@ -282,12 +301,11 @@
 
     scale = 4.0 / (best[0:1] + 1e-06)
     for x in range(across):
-        kappa = jnp.maximum(kappa_ref[0, x], averaged[x] * scale)
-        kappa_out[0, x] = kappa
-        grown = 1.0 - jnp.exp(-(kappa - 1.0) / 2.5) / kappa
         for y in range(along):
-            live = slots < counts_ref[0, x, y]
-            damage_out[0, x, pl.ds(y, 1), :] = jnp.where(live, grown[y : y + 1], 0.0)
+            kappa = jnp.maximum(kappa_ref[x, y], averaged[x, pl.ds(y, 1), :] * scale)
+            kappa_out[x, y] = kappa
+            live = slots < counts_ref[x, 0, y]
+            damage_out[x, y] = jnp.where(live, 1.0 - jnp.exp(-(kappa - 1.0) / 2.5) / kappa, 0.0)
 
 
 def on_device(sizes, coords, strain, kappa_old, counts, pair_mask):
@@ -299,9 +317,10 @@
     many = len(directions())
     targets = across * along
     slots = sizes[0] * sizes[1] + sizes[2]
-    return pl.pallas_call(
+    rows = jax.ShapeDtypeStruct((across, along, 1, points), jnp.float32)
+    kappa_new, damage = pl.pallas_call(
         functools.partial(damage_kernel, sizes),
-        out_shape=(jax.ShapeDtypeStruct(strain.shape, jnp.float32), jax.ShapeDtypeStruct(strain.shape, jnp.float32)),
+        out_shape=(rows, rows),
         in_specs=[smem, smem, vmem, vmem, vmem],
         out_specs=(vmem, vmem),
         scratch_shapes=[
@@ -318,7 +337,14 @@
             pltpu.SemaphoreType.DMA((slots,)),
         ],
         compiler_params=pltpu.CompilerParams(collective_id=0, has_side_effects=True, vmem_limit_bytes=FULL_VMEM),
-    )(counts, pair_mask, coords, strain, kappa_old)
+    )(
+        counts.transpose(1, 0, 2),
+        pair_mask.transpose(1, 2, 0, 3),
+        coords.transpose(0, 2, 3, 1, 4),
+        strain.transpose(1, 2, 0, 3),
+        kappa_old.transpose(1, 2, 0, 3),
+    )
+    return kappa_new.transpose(2, 0, 1, 3), damage.transpose(2, 0, 1, 3)
 
 
 def solution(mesh):

time: 37.6 us -> 34.9 us (0.928)
  Pallas kernels: 33.3 us -> 29 us
  local copies, waits for them, and re-layouts: 3.41 us -> 4.87 us
    pallas_call x1, Pallas kernels: 33.3 us -> 29 us  [on_device(): pl.pallas_call(functools.partial(damage_kernel, sizes), out_shape=(rows,...]
    unnamed x11 -> x12, local copies, waits for them, and re-layouts: 2.16 us -> 4.87 us
    pallas_call x2 -> x0, local copies, waits for them, and re-layouts: 1.25 us -> none  [on_device(): pl.pallas_call(functools.partial(damage_kernel, sizes), out_shape=(jax.Sh...]
where the time goes in v3:
time: 34.9 us; the launch traced here: 34.5 us
  Pallas kernels  29 us (83%)
  local copies, waits for them, and re-layouts  4.87 us (14%)
  between operations  0.65 us (2%)
    pallas_call x1, Pallas kernels, on_device(): pl.pallas_call(functools.partial(damage_kernel, sizes), out_shape=(rows,...  29 us
    unnamed x12, local copies, waits for them, and re-layouts  4.87 us

profile of v3, /device:TPU:0, one launch (start us, length us, event | category | flops | bytes accessed | tf_op | source)
XLA Modules:
  0.0 34.5 jit_solution(13308236892429114040)
XLA Ops:
  0.6 0.0 copy-start.4
  0.6 0.7 %copy-done.4 = s32[1,6,6]{2,0,1:T(1,128)S(1)} copy-done((s32[1,6,6]{2,0,1:T(1,128)S(1)}, s32[1,6,6]{2,0,1:T(1,128)}, u32[]{:S(2)}) %copy-start.4) | copy-done | bytes 168
  1.3 0.0 copy-start
  1.3 0.8 %copy-done = f32[3,1,6,6,128]{4,1,3,2,0:T(1,128)S(1)} copy-done((f32[3,1,6,6,128]{4,1,3,2,0:T(1,128)S(1)}, f32[3,1,6,6,128]{4,1,3,2,0:T(1,128)}, u32[]{:S(2)}) %copy-start) | copy-done | bytes 55320
  2.1 0.0 copy-start.1
  2.1 0.7 %copy-done.1 = s32[1,6,6,26]{3,0,2,1:T(1,128)S(1)} copy-done((s32[1,6,6,26]{3,0,2,1:T(1,128)S(1)}, s32[1,6,6,26]{3,0,2,1:T(1,128)}, u32[]{:S(2)}) %copy-start.1) | copy-done | bytes 3768
  2.9 0.0 copy-start.2
  2.9 0.7 %copy-done.2 = f32[1,6,6,128]{3,0,2,1:T(1,128)S(1)} copy-done((f32[1,6,6,128]{3,0,2,1:T(1,128)S(1)}, f32[1,6,6,128]{3,0,2,1:T(1,128)}, u32[]{:S(2)}) %copy-start.2) | copy-done | bytes 18456
  3.6 0.0 copy-start.3
  3.6 0.7 %copy-done.3 = f32[1,6,6,128]{3,0,2,1:T(1,128)S(1)} copy-done((f32[1,6,6,128]{3,0,2,1:T(1,128)S(1)}, f32[1,6,6,128]{3,0,2,1:T(1,128)}, u32[]{:S(2)}) %copy-start.3) | copy-done | bytes 18456
  4.3 29.0 %shard_map.68 = (f32[6,6,1,128]{3,2,1,0:T(1,128)S(1)}, f32[6,6,1,128]{3,2,1,0:T(1,128)S(1)}) custom-call(s32[6,1,6]{2,1,0:T(1,128)S(1)} %bitcast.13, s32[6,6,1,26]{3,2,1,0:T(1,128)S(1)} %bitcast.8, f32[3,6,6,1,128]{4,3,2,1,0:T(1,128)S(1)} %bitcast.7, f32[6,6,1,128]{3,2,1,0:T(1,128)S(1)} %bitcast.9, f32[6,6,1,128]{3,2,1,0:T(1,128)S(1)} %bitcast.10), custom_call_target="tpu_custom_call" | custom-call | tf_op jit(solution)/shard_map/pallas_call | solution.py:321
  33.3 0.6 %copy.9 = f32[1,6,6,128]{3,0,2,1:T(1,128)} copy(f32[1,6,6,128]{3,0,2,1:T(1,128)S(1)} %bitcast.12) | data formatting | bytes 36864
  33.9 0.6 %copy.10 = f32[1,6,6,128]{3,0,2,1:T(1,128)} copy(f32[1,6,6,128]{3,0,2,1:T(1,128)S(1)} %bitcast.11) | data formatting | bytes 36864
Async XLA Ops:
  0.6 0.7 %copy-start.4 = (s32[1,6,6]{2,0,1:T(1,128)S(1)}, s32[1,6,6]{2,0,1:T(1,128)}, u32[]{:S(2)}) copy-start(s32[1,6,6]{2,0,1:T(1,128)} %param.8) | copy-start | bytes 436
  1.3 0.8 %copy-start = (f32[3,1,6,6,128]{4,1,3,2,0:T(1,128)S(1)}, f32[3,1,6,6,128]{4,1,3,2,0:T(1,128)}, u32[]{:S(2)}) copy-start(f32[3,1,6,6,128]{4,1,3,2,0:T(1,128)} %param.5) | copy-start | bytes 165892
  2.1 0.7 %copy-start.1 = (s32[1,6,6,26]{3,0,2,1:T(1,128)S(1)}, s32[1,6,6,26]{3,0,2,1:T(1,128)}, u32[]{:S(2)}) copy-start(s32[1,6,6,26]{3,0,2,1:T(1,128)} %param.9) | copy-start | bytes 11236
  2.9 0.7 %copy-start.2 = (f32[1,6,6,128]{3,0,2,1:T(1,128)S(1)}, f32[1,6,6,128]{3,0,2,1:T(1,128)}, u32[]{:S(2)}) copy-start(f32[1,6,6,128]{3,0,2,1:T(1,128)} %param.6) | copy-start | bytes 55300
  3.6 0.7 %copy-start.3 = (f32[1,6,6,128]{3,0,2,1:T(1,128)S(1)}, f32[1,6,6,128]{3,0,2,1:T(1,128)}, u32[]{:S(2)}) copy-start(f32[1,6,6,128]{3,0,2,1:T(1,128)} %param.7) | copy-start | bytes 55300

commit v4 on v3

--- a/solution.py
+++ b/solution.py
@@ -10,10 +10,9 @@
 MESH = pl.DeviceIdType.MESH
 AXES = ("ply", "gx", "gy")
 FAR = -1e30
-ROWS = 64
-DEPTH = 32
-AHEAD = 2
-FULL_VMEM = 48 * 1024 * 1024
+DEPTH = 48
+AHEAD = 1
+FULL_VMEM = 58 * 1024 * 1024
 
 
 def directions():
@@ -34,10 +33,20 @@
     return {-1: (0, 1), 0: (1, size), 1: (size + 1, 1)}[step]
 
 
-def damage_kernel(sizes, counts_ref, mask_ref, coords_ref, strain_ref, kappa_ref, kappa_out, damage_out,
-                  pack, source, target_side, total_w, total_s, averaged, held, send_sem, recv_sem, max_send, max_recv):
+def damage_kernel(sizes, counts_in, mask_in, coords_in, strain_in, kappa_in, kappa_out, damage_out,
+                  counts_ref, mask_ref, coords_ref, strain_ref, kappa_ref, pack, source, shade, target_side,
+                  total_w, total_s, averaged, held, in_sem, send_sem, recv_sem, max_send, max_recv):
     across, along, _, points = strain_ref.shape
     wide, deep = across + 2, along + 2
+    staged = [
+        pltpu.make_async_copy(given, kept, in_sem.at[k])
+        for k, (given, kept) in enumerate(
+            [(counts_in, counts_ref), (coords_in, coords_ref), (strain_in, strain_ref), (mask_in, mask_ref),
+             (kappa_in, kappa_ref)]
+        )
+    ]
+    for copy in staged:
+        copy.start()
     ply, gx, gy = (lax.axis_index(axis) for axis in AXES)
     listed = directions()
 
@@ -69,6 +78,8 @@
             pl.semaphore_signal(barrier, inc=1, device_id=max_peer(which, index), device_id_type=MESH)
 
     slots = lax.broadcasted_iota(jnp.int32, (1, points), 1)
+    for copy in staged[:3]:
+        copy.wait()
     for x in range(across):
         for y in range(along):
             for comp in range(3):
@@ -103,7 +114,6 @@
     sub = lax.broadcasted_iota(jnp.int32, (8, points), 0)
     top = sub < 4
     row = jnp.where(top, sub, sub - 4)
-    last = jnp.where(top, 1.0, 0.0)
 
     def split(rows):
         high = rows.astype(jnp.bfloat16).astype(jnp.float32)
@@ -121,19 +131,46 @@
     def stack(rows):
         return jnp.where(row == 0, rows[0], jnp.where(row == 1, rows[1], jnp.where(row == 2, rows[2], rows[3])))
 
+    def kind(x, y):
+        return lax.rem(x, 3) * 3 + y % 3
+
     def build_source(layer, x, y, found, squared):
         strain = jnp.broadcast_to(pack[layer, x, y, pl.ds(3, 1), :], (8, points))
         high, middle, low = split(stack(found + [jnp.where(strain > 0.0, -squared, FAR)]))
         pair = jnp.where(top, high, middle)
-        rows = jnp.concatenate([pair, jnp.where(top, high, low), pair, last], 0)
-        source[layer, x, :, pl.ds(y * points, points)] = rows.astype(jnp.bfloat16)
+        fourth = jnp.where((sub < 3) | (sub - 4 == kind(x, y)), 1.0, 0.0)
+        fifth = jnp.where(sub + 4 == kind(x, y), 1.0, 0.0)
+        rows = jnp.concatenate([pair, jnp.where(top, high, low), pair, fourth, fifth, strain], 0).T
+        span = pl.ds(y * points, points)
+        source[layer, x, span, :] = rows.astype(jnp.bfloat16)
+        shade[layer, x, span, :] = jnp.broadcast_to(rows[:, DEPTH - 1 : DEPTH], (points, points))
+
+    mask_base = jnp.where(ply == 0, 17, 0)
 
     def build_target(x, y, found, squared):
         high, middle, low = split(stack([2.0 * spot for spot in found] + [jnp.ones((8, points), jnp.float32)]))
         a_high, a_middle, a_low = split(1.0 - squared)
-        own = jnp.where(sub == 0, a_high, jnp.where(sub == 1, a_middle, jnp.where(sub == 2, a_low, jnp.where(sub == 4, 1.0, 0.0))))
-        rows = jnp.concatenate([high, jnp.where(top, middle, high), jnp.where(top, low, middle), own], 0)
-        target_side[(x - 1) * along + y - 1] = rows.T.astype(jnp.bfloat16)
+        own = jnp.where(sub == 0, a_high, jnp.where(sub == 1, a_middle, jnp.where(sub == 2, a_low, 0.0)))
+        fixed = [high, jnp.where(top, middle, high), jnp.where(top, low, middle)]
+        zero = jnp.zeros((8, points), jnp.float32)
+        for layer in range(2):
+            fourth, fifth = own, zero
+            for which in range(9):
+                near = lax.rem(which // 3 - x + 1 + 3 * wide, 3) * 3 + (which % 3 - y + 1) % 3
+                if layer:
+                    flag = mask_ref[x - 1, y - 1, 0, mask_base + near]
+                else:
+                    flag = mask_ref[x - 1, y - 1, 0, 9 + near - (near > 4).astype(jnp.int32)]
+                    flag = jnp.where(near == 4, 1, flag)
+                away = FAR * (1 - flag).astype(jnp.float32)
+                if which < 4:
+                    fourth = jnp.where(sub == which + 4, away, fourth)
+                else:
+                    fifth = jnp.where(sub == which - 4, away, fifth)
+            rows = jnp.concatenate(fixed + [fourth, fifth, zero], 0)
+            target_side[layer, x - 1, :, pl.ds((y - 1) * points, points)] = rows.astype(jnp.bfloat16)
+
+    staged[3].wait()
 
     def own_row(x, carry):
         for y in range(1, along + 1):
@@ -144,58 +181,49 @@
 
     lax.fori_loop(1, across + 1, own_row, 0)
 
-    mask_base = jnp.where(ply == 0, 17, 0)
-
-    half_rows = lax.broadcasted_iota(jnp.int32, (DEPTH // 2, points), 0)
-    mask_row = jnp.where(half_rows == 12, 1.0, 0.0).astype(jnp.bfloat16)
-
-    def masked_source(layer, x, y, near):
-        block = source[layer, x + near // 3, :, pl.ds((y + near % 3) * points, points)]
-        if layer == 0 and near == 4:
-            return block
-        flag = mask_ref[x, y, 0, mask_base + near if layer else 9 + near - (near > 4)]
-        away = jnp.full(mask_row.shape, FAR * (1 - flag).astype(jnp.float32)).astype(jnp.bfloat16)
-        return jnp.concatenate([block[: DEPTH // 2], block[DEPTH // 2 :] + mask_row * away], 0)
-
-    def row_sums(x, ys, layer):
-        tasks = [(y, at, pair) for y in ys for at in range(0, points, ROWS) for pair in range(0, 9, 2)]
-        sides = {}
+    def fold(block):
+        return jnp.sum(block.reshape(points // 8, 8, points), axis=0)
+
+    def row_sums(x, groups, layer):
+        tasks = [(group, step) for group in groups for step in range(3)]
 
         def product(task):
-            y, at, pair = task
-            nears = [near for near in (pair, pair + 1) if near < 9]
-            for near in nears:
-                if (y, near) not in sides:
-                    sides[y, near] = masked_source(layer, x, y, near)
-            beside = jnp.concatenate([sides[y, near] for near in nears], axis=1)
-            rows = target_side[x * along + y, pl.ds(at, ROWS), :]
-            return nears, jnp.dot(rows, beside, preferred_element_type=jnp.float32)
+            (y, many), step = task
+            beside = source[layer, x + step, pl.ds(y * points, (many + 2) * points), :]
+            these = target_side[layer, x, :, pl.ds(y * points, many * points)]
+            return jnp.dot(beside, these, preferred_element_type=jnp.float32)
 
         ready = [product(task) for task in tasks[:AHEAD]]
-        sum_w = sum_s = None
-        for k, (y, at, pair) in enumerate(tasks):
+        sums = {}
+        for k, ((y, many), step) in enumerate(tasks):
             if k + AHEAD < len(tasks):
                 ready.append(product(tasks[k + AHEAD]))
-            nears, inside = ready.pop(0)
-            for slot, near in enumerate(nears):
-                weight = jnp.maximum(inside[:, slot * points : (slot + 1) * points], 0.0)
-                weight = weight * weight
-                term = weight * pack[layer, x + near // 3, y + near % 3, pl.ds(3, 1), :]
-                sum_w = weight if near == 0 else sum_w + weight
-                sum_s = term if near == 0 else sum_s + term
-            if pair == 8:
-                place = (x * along + y, pl.ds(at, ROWS))
-                if layer:
-                    sum_w = sum_w + total_w[place]
-                    sum_s = sum_s + total_s[place]
-                total_w[place] = sum_w
-                total_s[place] = sum_s
-
-    def own_layer(x, ys):
-        row_sums(x, ys, 0)
+            inside = ready.pop(0)
+            for block in range(many + 2):
+                tint = shade[layer, x + step, pl.ds((y + block) * points, points), :]
+                for one in range(many):
+                    if not 0 <= block - one <= 2:
+                        continue
+                    weight = inside[block * points : (block + 1) * points, one * points : (one + 1) * points]
+                    weight = jnp.maximum(weight, 0.0)
+                    weight = weight * weight
+                    sum_w, sum_s = sums.get((y, one), (0.0, 0.0))
+                    sums[y, one] = (sum_w + fold(weight), sum_s + fold(weight * tint))
+            if step == 2:
+                for one in range(many):
+                    sum_w, sum_s = sums[y, one]
+                    target = x * along + y + one
+                    if layer:
+                        sum_w = sum_w + total_w[target]
+                        sum_s = sum_s + total_s[target]
+                    total_w[target] = sum_w
+                    total_s[target] = sum_s
+
+    def pairs(start, stop):
+        return [(y, min(2, stop - y)) for y in range(start, stop, 2)]
 
     def inner_row(x, carry):
-        own_layer(x, range(1, along - 1))
+        row_sums(x, pairs(1, along - 1), 0)
         return carry
 
     lax.fori_loop(1, across - 1, inner_row, 0)
@@ -235,43 +263,28 @@
     lax.fori_loop(0, 2, halo_end, 0)
 
     def edge_row(x, carry):
-        own_layer(x, (0, along - 1))
+        row_sums(x, [(0, 1), (along - 1, 1)], 0)
         return carry
 
     def end_row(end, carry):
-        own_layer(end * (across - 1), range(along))
+        row_sums(end * (across - 1), pairs(0, along), 0)
+        return carry
+
+    def other_layer(x, carry):
+        row_sums(x, pairs(0, along), 1)
         return carry
 
     lax.fori_loop(1, across - 1, edge_row, 0)
     lax.fori_loop(0, 2, end_row, 0)
-
-    def other_layer(x, carry):
-        row_sums(x, range(along), 1)
-        return carry
-
     lax.fori_loop(0, across, other_layer, 0)
 
-    ones = jnp.ones((8, 2 * points), jnp.bfloat16)
-
-    def lane_sums(block):
-        high = block.astype(jnp.bfloat16)
-        low = (block - high.astype(jnp.float32)).astype(jnp.bfloat16)
-        both = jnp.concatenate([high, low], axis=1)
-        summed = lax.dot_general(ones, both, (((1,), (1,)), ((), ())), preferred_element_type=jnp.float32)
-        return summed[0:1]
-
-    def divide(x, carry):
-        these = pl.ds(x * along, along)
-        weight_sum = lane_sums(total_w[these].reshape(along * points, points))
-        weighted = lane_sums(total_s[these].reshape(along * points, points))
+    for x in range(across):
         for y in range(along):
-            span = slice(y * points, (y + 1) * points)
+            weight_sum = jnp.sum(total_w[x * along + y], axis=0, keepdims=True)
+            weighted = jnp.sum(total_s[x * along + y], axis=0, keepdims=True)
             live = slots < counts_ref[x, 0, y]
-            share = weighted[:, span] / jnp.where(live, weight_sum[:, span], 1.0)
+            share = weighted / jnp.where(live, weight_sum, 1.0)
             averaged[x, pl.ds(y, 1), :] = jnp.where(live, share, 0.0)
-        return carry
-
-    lax.fori_loop(0, across, divide, 0)
 
     best = jnp.max(averaged[...])
     at = 0
@@ -299,6 +312,7 @@
         best = best if which else jnp.max(best)
         at += len(rounds[which]) + 1
 
+    staged[4].wait()
     scale = 4.0 / (best[0:1] + 1e-06)
     for x in range(across):
         for y in range(along):
@@ -313,7 +327,6 @@
     assert layers == 1 and sizes[0] == 2
     wide, deep = across + 2, along + 2
     vmem = pl.BlockSpec(memory_space=pltpu.VMEM)
-    smem = pl.BlockSpec(memory_space=pltpu.SMEM)
     many = len(directions())
     targets = across * along
     slots = sizes[0] * sizes[1] + sizes[2]
@@ -321,16 +334,23 @@
     kappa_new, damage = pl.pallas_call(
         functools.partial(damage_kernel, sizes),
         out_shape=(rows, rows),
-        in_specs=[smem, smem, vmem, vmem, vmem],
+        in_specs=[pl.BlockSpec(memory_space=pl.ANY)] * 5,
         out_specs=(vmem, vmem),
         scratch_shapes=[
+            pltpu.SMEM((across, 1, along), jnp.int32),
+            pltpu.SMEM((across, along, 1, pair_mask.shape[3]), jnp.int32),
+            pltpu.VMEM((3, across, along, 1, points), jnp.float32),
+            pltpu.VMEM((across, along, 1, points), jnp.float32),
+            pltpu.VMEM((across, along, 1, points), jnp.float32),
             pltpu.VMEM((2, wide, deep, 4, points), jnp.float32),
-            pltpu.VMEM((2, wide, DEPTH, deep * points), jnp.bfloat16),
-            pltpu.VMEM((targets, points, DEPTH), jnp.bfloat16),
-            pltpu.VMEM((targets, points, points), jnp.float32),
-            pltpu.VMEM((targets, points, points), jnp.float32),
+            pltpu.VMEM((2, wide, deep * points, DEPTH), jnp.bfloat16),
+            pltpu.VMEM((2, wide, deep * points, points), jnp.float32),
+            pltpu.VMEM((2, across, DEPTH, along * points), jnp.bfloat16),
+            pltpu.VMEM((targets, 8, points), jnp.float32),
+            pltpu.VMEM((targets, 8, points), jnp.float32),
             pltpu.VMEM((across, along, points), jnp.float32),
             pltpu.VMEM((slots, 8, points), jnp.float32),
+            pltpu.SemaphoreType.DMA((5,)),
             pltpu.SemaphoreType.DMA((many,)),
             pltpu.SemaphoreType.DMA((many,)),
             pltpu.SemaphoreType.DMA((slots,)),

time: 34.9 us -> 33.3 us (0.954)
  local copies, waits for them, and re-layouts: 4.87 us -> 1.95 us
  Pallas kernels: 29 us -> 30.4 us
    unnamed x12 -> x4, local copies, waits for them, and re-layouts: 4.87 us -> 1.95 us
    pallas_call x1, Pallas kernels: 29 us -> 30.4 us  [on_device(): pl.pallas_call(functools.partial(damage_kernel, sizes), out_shape=(rows,...]
where the time goes in v4:
time: 33.3 us; the launch traced here: 33 us
  Pallas kernels  30.4 us (91%)
  local copies, waits for them, and re-layouts  1.95 us (6%)
  between operations  0.65 us (2%)
    pallas_call x1, Pallas kernels, on_device(): pl.pallas_call(functools.partial(damage_kernel, sizes), out_shape=(rows,...  30.4 us
    unnamed x4, local copies, waits for them, and re-layouts  1.95 us

profile of v4, /device:TPU:0, one launch (start us, length us, event | category | flops | bytes accessed | tf_op | source)
XLA Modules:
  0.0 33.0 jit_solution(629832745050031458)
XLA Ops:
  0.6 30.4 %shard_map.68 = (f32[6,6,1,128]{3,2,1,0:T(1,128)}, f32[6,6,1,128]{3,2,1,0:T(1,128)}) custom-call(s32[6,1,6]{2,1,0:T(1,128)} %bitcast.13, s32[6,6,1,26]{3,2,1,0:T(1,128)} %bitcast.8, f32[3,6,6,1,128]{4,3,2,1,0:T(1,128)} %bitcast.7, f32[6,6,1,128]{3,2,1,0:T(1,128)} %bitcast.9, f32[6,6,1,128]{3,2,1,0:T(1,128)} %bitcast.10), custom_call_target="tpu_custom_call" | custom-call | tf_op jit(solution)/shard_map/pallas_call | solution.py:334
  31.1 0.0 copy-start
  31.1 1.3 %copy.9 = f32[1,6,6,128]{3,0,2,1:T(1,128)} copy(f32[1,6,6,128]{3,0,2,1:T(1,128)} %bitcast.12) | data formatting | bytes 36864
  32.4 0.0 copy-done
  32.4 0.6 %copy.10 = f32[1,6,6,128]{3,0,2,1:T(1,128)} copy(f32[1,6,6,128]{3,0,2,1:T(1,128)S(1)} %bitcast.11) | data formatting | bytes 36864
Async XLA Ops:
  31.1 1.4 %copy-start = (f32[6,6,1,128]{3,2,1,0:T(1,128)S(1)}, f32[6,6,1,128]{3,2,1,0:T(1,128)}, u32[]{:S(2)}) copy-start(f32[6,6,1,128]{3,2,1,0:T(1,128)} %get-tuple-element.5) | copy-start | bytes 55300

commit v5 on v3

--- a/solution.py
+++ b/solution.py
@@ -10,10 +10,10 @@
 MESH = pl.DeviceIdType.MESH
 AXES = ("ply", "gx", "gy")
 FAR = -1e30
-ROWS = 64
+ROWS = 128
 DEPTH = 32
-AHEAD = 2
-FULL_VMEM = 48 * 1024 * 1024
+AHEAD = 1
+FULL_VMEM = 58 * 1024 * 1024
 
 
 def directions():
@@ -34,10 +34,19 @@
     return {-1: (0, 1), 0: (1, size), 1: (size + 1, 1)}[step]
 
 
-def damage_kernel(sizes, counts_ref, mask_ref, coords_ref, strain_ref, kappa_ref, kappa_out, damage_out,
-                  pack, source, target_side, total_w, total_s, averaged, held, send_sem, recv_sem, max_send, max_recv):
+def average_kernel(sizes, counts_in, mask_in, coords_in, strain_in, out_ref,
+                   counts_ref, mask_ref, coords_ref, strain_ref, pack, source, target_side,
+                   total_w, total_s, averaged, held, in_sem, send_sem, recv_sem, max_send, max_recv):
     across, along, _, points = strain_ref.shape
     wide, deep = across + 2, along + 2
+    staged = [
+        pltpu.make_async_copy(given, kept, in_sem.at[k])
+        for k, (given, kept) in enumerate(
+            [(counts_in, counts_ref), (coords_in, coords_ref), (strain_in, strain_ref), (mask_in, mask_ref)]
+        )
+    ]
+    for copy in staged:
+        copy.start()
     ply, gx, gy = (lax.axis_index(axis) for axis in AXES)
     listed = directions()
 
@@ -69,6 +78,8 @@
             pl.semaphore_signal(barrier, inc=1, device_id=max_peer(which, index), device_id_type=MESH)
 
     slots = lax.broadcasted_iota(jnp.int32, (1, points), 1)
+    for copy in staged[:3]:
+        copy.wait()
     for x in range(across):
         for y in range(along):
             for comp in range(3):
@@ -144,6 +155,7 @@
 
     lax.fori_loop(1, across + 1, own_row, 0)
 
+    staged[3].wait()
     mask_base = jnp.where(ply == 0, 17, 0)
 
     half_rows = lax.broadcasted_iota(jnp.int32, (DEPTH // 2, points), 0)
@@ -299,13 +311,11 @@
         best = best if which else jnp.max(best)
         at += len(rounds[which]) + 1
 
-    scale = 4.0 / (best[0:1] + 1e-06)
+    highest = best[0:1] + 1e-06
     for x in range(across):
         for y in range(along):
-            kappa = jnp.maximum(kappa_ref[x, y], averaged[x, pl.ds(y, 1), :] * scale)
-            kappa_out[x, y] = kappa
-            live = slots < counts_ref[x, 0, y]
-            damage_out[x, y] = jnp.where(live, 1.0 - jnp.exp(-(kappa - 1.0) / 2.5) / kappa, 0.0)
+            scaled = 4.0 * averaged[x, pl.ds(y, 1), :] / highest
+            out_ref[x, y] = jnp.where(slots < counts_ref[x, 0, y], scaled, -1.0)
 
 
 def on_device(sizes, coords, strain, kappa_old, counts, pair_mask):
@@ -313,17 +323,19 @@
     assert layers == 1 and sizes[0] == 2
     wide, deep = across + 2, along + 2
     vmem = pl.BlockSpec(memory_space=pltpu.VMEM)
-    smem = pl.BlockSpec(memory_space=pltpu.SMEM)
     many = len(directions())
     targets = across * along
     slots = sizes[0] * sizes[1] + sizes[2]
-    rows = jax.ShapeDtypeStruct((across, along, 1, points), jnp.float32)
-    kappa_new, damage = pl.pallas_call(
-        functools.partial(damage_kernel, sizes),
-        out_shape=(rows, rows),
-        in_specs=[smem, smem, vmem, vmem, vmem],
-        out_specs=(vmem, vmem),
+    scaled = pl.pallas_call(
+        functools.partial(average_kernel, sizes),
+        out_shape=jax.ShapeDtypeStruct((across, along, 1, points), jnp.float32),
+        in_specs=[pl.BlockSpec(memory_space=pl.ANY)] * 4,
+        out_specs=vmem,
         scratch_shapes=[
+            pltpu.SMEM((across, 1, along), jnp.int32),
+            pltpu.SMEM((across, along, 1, pair_mask.shape[3]), jnp.int32),
+            pltpu.VMEM((3, across, along, 1, points), jnp.float32),
+            pltpu.VMEM((across, along, 1, points), jnp.float32),
             pltpu.VMEM((2, wide, deep, 4, points), jnp.float32),
             pltpu.VMEM((2, wide, DEPTH, deep * points), jnp.bfloat16),
             pltpu.VMEM((targets, points, DEPTH), jnp.bfloat16),
@@ -331,6 +343,7 @@
             pltpu.VMEM((targets, points, points), jnp.float32),
             pltpu.VMEM((across, along, points), jnp.float32),
             pltpu.VMEM((slots, 8, points), jnp.float32),
+            pltpu.SemaphoreType.DMA((4,)),
             pltpu.SemaphoreType.DMA((many,)),
             pltpu.SemaphoreType.DMA((many,)),
             pltpu.SemaphoreType.DMA((slots,)),
@@ -342,9 +355,11 @@
         pair_mask.transpose(1, 2, 0, 3),
         coords.transpose(0, 2, 3, 1, 4),
         strain.transpose(1, 2, 0, 3),
-        kappa_old.transpose(1, 2, 0, 3),
     )
-    return kappa_new.transpose(2, 0, 1, 3), damage.transpose(2, 0, 1, 3)
+    scaled = scaled.transpose(2, 0, 1, 3)
+    kappa_new = jnp.maximum(kappa_old, scaled)
+    damage = jnp.where(scaled < 0.0, 0.0, 1.0 - jnp.exp(-(kappa_new - 1.0) / 2.5) / kappa_new)
+    return kappa_new, damage
 
 
 def solution(mesh):

time: 34.9 us -> 31.1 us (0.89)
  local copies, waits for them, and re-layouts: 4.87 us -> 0.01 us
  other arithmetic: 0 us -> 1.39 us
    unnamed x12 -> x2, local copies, waits for them, and re-layouts: 4.87 us -> 0.01 us
    select_n x0 -> x1, other arithmetic: none -> 1.39 us  [on_device(): jnp.where(scaled < 0.0, 0.0, 1.0 - jnp.exp(-(kappa_new - 1.0) / 2.5) / ka...]
where the time goes in v5:
time: 31.1 us; the launch traced here: 30.9 us
  Pallas kernels  28.9 us (93%)
  other arithmetic  1.39 us (4%)
  between operations  0.66 us (2%)
    pallas_call x1, Pallas kernels, on_device(): pl.pallas_call(functools.partial(average_kernel, sizes), out_shape=jax.Sh...  28.9 us
    select_n x1, other arithmetic, on_device(): jnp.where(scaled < 0.0, 0.0, 1.0 - jnp.exp(-(kappa_new - 1.0) / 2.5) / ka...  1.39 us

profile of v5, /device:TPU:0, one launch (start us, length us, event | category | flops | bytes accessed | tf_op | source)
XLA Modules:
  0.0 30.9 jit_solution(1316062159029082757)
XLA Ops:
  0.6 0.0 copy-start
  0.6 28.9 %shard_map.68 = f32[6,6,1,128]{3,2,1,0:T(1,128)} custom-call(s32[6,1,6]{2,1,0:T(1,128)} %bitcast.11, s32[6,6,1,26]{3,2,1,0:T(1,128)} %bitcast.9, f32[3,6,6,1,128]{4,3,2,1,0:T(1,128)} %bitcast.8, f32[6,6,1,128]{3,2,1,0:T(1,128)} %bitcast.10), custom_call_target="tpu_custom_call" | custom-call | tf_op jit(solution)/shard_map/pallas_call | solution.py:329
  29.5 0.0 copy-done
  29.5 1.4 %compare_select_fusion = (f32[1,6,6,128]{3,0,2,1:T(1,128)}, f32[1,6,6,128]{3,0,2,1:T(1,128)}) fusion(f32[6,6,1,128]{3,2,1,0:T(1,128)} %shard_map.68, f32[1,6,6,128]{3,0,2,1:T(1,128)S(1)} %copy-done), kind=kLoop, calls=%fused_computation | loop fusion | flops 36864 | bytes 73728 | tf_op jit(solution)/shard_map/jit(_where)/select_n | solution.py:361
Async XLA Ops:
  0.6 28.9 %copy-start = (f32[1,6,6,128]{3,0,2,1:T(1,128)S(1)}, f32[1,6,6,128]{3,0,2,1:T(1,128)}, u32[]{:S(2)}) copy-start(f32[1,6,6,128]{3,0,2,1:T(1,128)} %param.7) | copy-start | bytes 55300

commit v6 on v5

--- a/solution.py
+++ b/solution.py
@@ -10,7 +10,7 @@
 MESH = pl.DeviceIdType.MESH
 AXES = ("ply", "gx", "gy")
 FAR = -1e30
-ROWS = 128
+CHUNK = 32
 DEPTH = 32
 AHEAD = 1
 FULL_VMEM = 58 * 1024 * 1024
@@ -35,7 +35,7 @@
 
 
 def average_kernel(sizes, counts_in, mask_in, coords_in, strain_in, out_ref,
-                   counts_ref, mask_ref, coords_ref, strain_ref, pack, source, target_side,
+                   counts_ref, mask_ref, coords_ref, strain_ref, pack, plain, source, target_side, column,
                    total_w, total_s, averaged, held, in_sem, send_sem, recv_sem, max_send, max_recv):
     across, along, _, points = strain_ref.shape
     wide, deep = across + 2, along + 2
@@ -134,7 +134,9 @@
 
     def build_source(layer, x, y, found, squared):
         strain = jnp.broadcast_to(pack[layer, x, y, pl.ds(3, 1), :], (8, points))
-        high, middle, low = split(stack(found + [jnp.where(strain > 0.0, -squared, FAR)]))
+        rows = stack(found + [jnp.where(strain > 0.0, -squared, FAR)])
+        plain[layer, x, y] = rows[:4]
+        high, middle, low = split(rows)
         pair = jnp.where(top, high, middle)
         rows = jnp.concatenate([pair, jnp.where(top, high, low), pair, last], 0)
         source[layer, x, :, pl.ds(y * points, points)] = rows.astype(jnp.bfloat16)
@@ -143,8 +145,12 @@
         high, middle, low = split(stack([2.0 * spot for spot in found] + [jnp.ones((8, points), jnp.float32)]))
         a_high, a_middle, a_low = split(1.0 - squared)
         own = jnp.where(sub == 0, a_high, jnp.where(sub == 1, a_middle, jnp.where(sub == 2, a_low, jnp.where(sub == 4, 1.0, 0.0))))
-        rows = jnp.concatenate([high, jnp.where(top, middle, high), jnp.where(top, low, middle), own], 0)
-        target_side[(x - 1) * along + y - 1] = rows.T.astype(jnp.bfloat16)
+        twice = stack([2.0 * spot for spot in found] + [1.0 - squared])
+        rows = jnp.concatenate([high, jnp.where(top, middle, high), jnp.where(top, low, middle), own, twice], 0).T
+        target = (x - 1) * along + y - 1
+        target_side[target] = rows[:, :DEPTH].astype(jnp.bfloat16)
+        for comp in range(4):
+            column[target, comp] = jnp.broadcast_to(rows[:, DEPTH + comp : DEPTH + comp + 1], (points, points))
 
     def own_row(x, carry):
         for y in range(1, along + 1):
@@ -161,47 +167,60 @@
     half_rows = lax.broadcasted_iota(jnp.int32, (DEPTH // 2, points), 0)
     mask_row = jnp.where(half_rows == 12, 1.0, 0.0).astype(jnp.bfloat16)
 
+    def away_from(layer, x, y, near):
+        flag = mask_ref[x, y, 0, mask_base + near if layer else 9 + near - (near > 4)]
+        return FAR * (1 - flag).astype(jnp.float32)
+
     def masked_source(layer, x, y, near):
         block = source[layer, x + near // 3, :, pl.ds((y + near % 3) * points, points)]
         if layer == 0 and near == 4:
             return block
-        flag = mask_ref[x, y, 0, mask_base + near if layer else 9 + near - (near > 4)]
-        away = jnp.full(mask_row.shape, FAR * (1 - flag).astype(jnp.float32)).astype(jnp.bfloat16)
+        away = jnp.full(mask_row.shape, away_from(layer, x, y, near)).astype(jnp.bfloat16)
         return jnp.concatenate([block[: DEPTH // 2], block[DEPTH // 2 :] + mask_row * away], 0)
 
     def row_sums(x, ys, layer):
-        tasks = [(y, at, pair) for y in ys for at in range(0, points, ROWS) for pair in range(0, 9, 2)]
-        sides = {}
+        tasks = [(y, step) for y in ys for step in range(3)]
 
         def product(task):
-            y, at, pair = task
-            nears = [near for near in (pair, pair + 1) if near < 9]
-            for near in nears:
-                if (y, near) not in sides:
-                    sides[y, near] = masked_source(layer, x, y, near)
-            beside = jnp.concatenate([sides[y, near] for near in nears], axis=1)
-            rows = target_side[x * along + y, pl.ds(at, ROWS), :]
-            return nears, jnp.dot(rows, beside, preferred_element_type=jnp.float32)
-
+            y, step = task
+            beside = jnp.concatenate([masked_source(layer, x, y, 3 * step + slot) for slot in range(2)], axis=1)
+            return jnp.dot(target_side[x * along + y], beside, preferred_element_type=jnp.float32)
+
+        def add(at, inside, near, y):
+            weight = jnp.maximum(inside, 0.0)
+            weight = weight * weight
+            term = weight * pack[layer, x + near // 3, y + near % 3, pl.ds(3, 1), :]
+            sums[at] = (sums[at][0] + weight, sums[at][1] + term) if at in sums else (weight, term)
+
+        def direct(at, y):
+            spot = [column[x * along + y, comp, pl.ds(at, CHUNK), :] for comp in range(4)]
+            for near in (2, 5, 8):
+                row = [plain[layer, x + near // 3, y + 2, pl.ds(comp, 1), :] for comp in range(4)]
+                fixed = row[3] + away_from(layer, x, y, near)
+                add(at, spot[0] * row[0] + spot[1] * row[1] + (spot[2] * row[2] + (spot[3] + fixed)), near, y)
+
+        spans = range(0, points, CHUNK)
         ready = [product(task) for task in tasks[:AHEAD]]
-        sum_w = sum_s = None
-        for k, (y, at, pair) in enumerate(tasks):
+        for k, (y, step) in enumerate(tasks):
+            if step == 0:
+                sums = {}
             if k + AHEAD < len(tasks):
                 ready.append(product(tasks[k + AHEAD]))
-            nears, inside = ready.pop(0)
-            for slot, near in enumerate(nears):
-                weight = jnp.maximum(inside[:, slot * points : (slot + 1) * points], 0.0)
-                weight = weight * weight
-                term = weight * pack[layer, x + near // 3, y + near % 3, pl.ds(3, 1), :]
-                sum_w = weight if near == 0 else sum_w + weight
-                sum_s = term if near == 0 else sum_s + term
-            if pair == 8:
-                place = (x * along + y, pl.ds(at, ROWS))
-                if layer:
-                    sum_w = sum_w + total_w[place]
-                    sum_s = sum_s + total_s[place]
-                total_w[place] = sum_w
-                total_s[place] = sum_s
+            for at in list(spans)[step :: 3]:
+                direct(at, y)
+            inside = ready.pop(0)
+            for at in spans:
+                for slot in range(2):
+                    add(at, inside[at : at + CHUNK, slot * points : (slot + 1) * points], 3 * step + slot, y)
+            if step == 2:
+                for at in spans:
+                    place = (x * along + y, pl.ds(at, CHUNK))
+                    sum_w, sum_s = sums[at]
+                    if layer:
+                        sum_w = sum_w + total_w[place]
+                        sum_s = sum_s + total_s[place]
+                    total_w[place] = sum_w
+                    total_s[place] = sum_s
 
     def own_layer(x, ys):
         row_sums(x, ys, 0)
@@ -337,8 +356,10 @@
             pltpu.VMEM((3, across, along, 1, points), jnp.float32),
             pltpu.VMEM((across, along, 1, points), jnp.float32),
             pltpu.VMEM((2, wide, deep, 4, points), jnp.float32),
+            pltpu.VMEM((2, wide, deep, 4, points), jnp.float32),
             pltpu.VMEM((2, wide, DEPTH, deep * points), jnp.bfloat16),
             pltpu.VMEM((targets, points, DEPTH), jnp.bfloat16),
+            pltpu.VMEM((targets, 4, points, points), jnp.float32),
             pltpu.VMEM((targets, points, points), jnp.float32),
             pltpu.VMEM((targets, points, points), jnp.float32),
             pltpu.VMEM((across, along, points), jnp.float32),

time: 31.1 us -> 34.6 us (1.11)
  Pallas kernels: 28.9 us -> 32.3 us
    pallas_call x1, Pallas kernels: 28.9 us -> 32.3 us  [on_device(): pl.pallas_call(functools.partial(average_kernel, sizes), out_shape=jax.Sh...]
where the time goes in v6:
time: 34.6 us; the launch traced here: 34.4 us
  Pallas kernels  32.3 us (93%)
  other arithmetic  1.39 us (4%)
  between operations  0.66 us (2%)
    pallas_call x1, Pallas kernels, on_device(): pl.pallas_call(functools.partial(average_kernel, sizes), out_shape=jax.Sh...  32.3 us
    select_n x1, other arithmetic, on_device(): jnp.where(scaled < 0.0, 0.0, 1.0 - jnp.exp(-(kappa_new - 1.0) / 2.5) / ka...  1.39 us

profile of v6, /device:TPU:0, one launch (start us, length us, event | category | flops | bytes accessed | tf_op | source)
XLA Modules:
  0.0 34.4 jit_solution(5801307672858538644)
XLA Ops:
  0.6 0.0 copy-start
  0.6 32.3 %shard_map.68 = f32[6,6,1,128]{3,2,1,0:T(1,128)} custom-call(s32[6,1,6]{2,1,0:T(1,128)} %bitcast.11, s32[6,6,1,26]{3,2,1,0:T(1,128)} %bitcast.9, f32[3,6,6,1,128]{4,3,2,1,0:T(1,128)} %bitcast.8, f32[6,6,1,128]{3,2,1,0:T(1,128)} %bitcast.10), custom_call_target="tpu_custom_call" | custom-call | tf_op jit(solution)/shard_map/pallas_call | solution.py:348
  33.0 0.0 copy-done
  33.0 1.4 %compare_select_fusion = (f32[1,6,6,128]{3,0,2,1:T(1,128)}, f32[1,6,6,128]{3,0,2,1:T(1,128)}) fusion(f32[6,6,1,128]{3,2,1,0:T(1,128)} %shard_map.68, f32[1,6,6,128]{3,0,2,1:T(1,128)S(1)} %copy-done), kind=kLoop, calls=%fused_computation | loop fusion | flops 36864 | bytes 73728 | tf_op jit(solution)/shard_map/jit(_where)/select_n | solution.py:382
Async XLA Ops:
  0.6 32.3 %copy-start = (f32[1,6,6,128]{3,0,2,1:T(1,128)S(1)}, f32[1,6,6,128]{3,0,2,1:T(1,128)}, u32[]{:S(2)}) copy-start(f32[1,6,6,128]{3,0,2,1:T(1,128)} %param.7) | copy-start | bytes 55300

commit v7 on v5

--- a/solution.py
+++ b/solution.py
@@ -10,7 +10,7 @@
 MESH = pl.DeviceIdType.MESH
 AXES = ("ply", "gx", "gy")
 FAR = -1e30
-ROWS = 128
+ROWS = 32
 DEPTH = 32
 AHEAD = 1
 FULL_VMEM = 58 * 1024 * 1024
@@ -153,7 +153,7 @@
             build_target(x, y, found, squared)
         return carry
 
-    lax.fori_loop(1, across + 1, own_row, 0)
+    lax.fori_loop(1, across + 1, own_row, 0, unroll=2)
 
     staged[3].wait()
     mask_base = jnp.where(ply == 0, 17, 0)
@@ -170,32 +170,23 @@
         return jnp.concatenate([block[: DEPTH // 2], block[DEPTH // 2 :] + mask_row * away], 0)
 
     def row_sums(x, ys, layer):
-        tasks = [(y, at, pair) for y in ys for at in range(0, points, ROWS) for pair in range(0, 9, 2)]
-        sides = {}
-
-        def product(task):
-            y, at, pair = task
-            nears = [near for near in (pair, pair + 1) if near < 9]
-            for near in nears:
-                if (y, near) not in sides:
-                    sides[y, near] = masked_source(layer, x, y, near)
-            beside = jnp.concatenate([sides[y, near] for near in nears], axis=1)
-            rows = target_side[x * along + y, pl.ds(at, ROWS), :]
-            return nears, jnp.dot(rows, beside, preferred_element_type=jnp.float32)
-
-        ready = [product(task) for task in tasks[:AHEAD]]
-        sum_w = sum_s = None
-        for k, (y, at, pair) in enumerate(tasks):
-            if k + AHEAD < len(tasks):
-                ready.append(product(tasks[k + AHEAD]))
-            nears, inside = ready.pop(0)
-            for slot, near in enumerate(nears):
-                weight = jnp.maximum(inside[:, slot * points : (slot + 1) * points], 0.0)
-                weight = weight * weight
-                term = weight * pack[layer, x + near // 3, y + near % 3, pl.ds(3, 1), :]
-                sum_w = weight if near == 0 else sum_w + weight
-                sum_s = term if near == 0 else sum_s + term
-            if pair == 8:
+        def product(y):
+            beside = jnp.concatenate([masked_source(layer, x, y, near) for near in range(9)], axis=1)
+            return jnp.dot(target_side[x * along + y], beside, preferred_element_type=jnp.float32)
+
+        ready = [product(y) for y in ys[:AHEAD]]
+        for k, y in enumerate(ys):
+            if k + AHEAD < len(ys):
+                ready.append(product(ys[k + AHEAD]))
+            inside = ready.pop(0)
+            for at in range(0, points, ROWS):
+                sum_w = sum_s = None
+                for near in range(9):
+                    weight = jnp.maximum(inside[at : at + ROWS, near * points : (near + 1) * points], 0.0)
+                    weight = weight * weight
+                    term = weight * pack[layer, x + near // 3, y + near % 3, pl.ds(3, 1), :]
+                    sum_w = weight if near == 0 else sum_w + weight
+                    sum_s = term if near == 0 else sum_s + term
                 place = (x * along + y, pl.ds(at, ROWS))
                 if layer:
                     sum_w = sum_w + total_w[place]
@@ -243,8 +234,8 @@
             build_source(0, x, y, *spots(0, x, y))
         return carry
 
-    lax.fori_loop(0, wide, halo_row, 0)
-    lax.fori_loop(0, 2, halo_end, 0)
+    lax.fori_loop(0, wide, halo_row, 0, unroll=2)
+    lax.fori_loop(0, 2, halo_end, 0, unroll=2)
 
     def edge_row(x, carry):
         own_layer(x, (0, along - 1))
@@ -283,7 +274,8 @@
             averaged[x, pl.ds(y, 1), :] = jnp.where(live, share, 0.0)
         return carry
 
-    lax.fori_loop(0, across, divide, 0)
+    for x in range(across):
+        divide(x, 0)
 
     best = jnp.max(averaged[...])
     at = 0

time: 31.1 us -> 30.4 us (0.977)
  Pallas kernels: 28.9 us -> 28.2 us
    pallas_call x1, Pallas kernels: 28.9 us -> 28.2 us  [on_device(): pl.pallas_call(functools.partial(average_kernel, sizes), out_shape=jax.Sh...]
where the time goes in v7:
time: 30.4 us; the launch traced here: 30.2 us
  Pallas kernels  28.2 us (93%)
  other arithmetic  1.39 us (5%)
  between operations  0.66 us (2%)
    pallas_call x1, Pallas kernels, on_device(): pl.pallas_call(functools.partial(average_kernel, sizes), out_shape=jax.Sh...  28.2 us
    select_n x1, other arithmetic, on_device(): jnp.where(scaled < 0.0, 0.0, 1.0 - jnp.exp(-(kappa_new - 1.0) / 2.5) / ka...  1.39 us

profile of v7, /device:TPU:0, one launch (start us, length us, event | category | flops | bytes accessed | tf_op | source)
XLA Modules:
  0.0 30.2 jit_solution(16568389046486073970)
XLA Ops:
  0.6 0.0 copy-start
  0.6 28.2 %shard_map.68 = f32[6,6,1,128]{3,2,1,0:T(1,128)} custom-call(s32[6,1,6]{2,1,0:T(1,128)} %bitcast.11, s32[6,6,1,26]{3,2,1,0:T(1,128)} %bitcast.9, f32[3,6,6,1,128]{4,3,2,1,0:T(1,128)} %bitcast.8, f32[6,6,1,128]{3,2,1,0:T(1,128)} %bitcast.10), custom_call_target="tpu_custom_call" | custom-call | tf_op jit(solution)/shard_map/pallas_call | solution.py:321
  28.8 0.0 copy-done
  28.8 1.4 %compare_select_fusion = (f32[1,6,6,128]{3,0,2,1:T(1,128)}, f32[1,6,6,128]{3,0,2,1:T(1,128)}) fusion(f32[6,6,1,128]{3,2,1,0:T(1,128)} %shard_map.68, f32[1,6,6,128]{3,0,2,1:T(1,128)S(1)} %copy-done), kind=kLoop, calls=%fused_computation | loop fusion | flops 36864 | bytes 73728 | tf_op jit(solution)/shard_map/jit(_where)/select_n | solution.py:353
Async XLA Ops:
  0.6 28.2 %copy-start = (f32[1,6,6,128]{3,0,2,1:T(1,128)S(1)}, f32[1,6,6,128]{3,0,2,1:T(1,128)}, u32[]{:S(2)}) copy-start(f32[1,6,6,128]{3,0,2,1:T(1,128)} %param.7) | copy-start | bytes 55300

commit v8 on v7

--- a/solution.py
+++ b/solution.py
@@ -169,15 +169,16 @@
         away = jnp.full(mask_row.shape, FAR * (1 - flag).astype(jnp.float32)).astype(jnp.bfloat16)
         return jnp.concatenate([block[: DEPTH // 2], block[DEPTH // 2 :] + mask_row * away], 0)
 
-    def row_sums(x, ys, layer):
-        def product(y):
+    def row_sums(x, jobs):
+        def product(job):
+            y, layer = job
             beside = jnp.concatenate([masked_source(layer, x, y, near) for near in range(9)], axis=1)
             return jnp.dot(target_side[x * along + y], beside, preferred_element_type=jnp.float32)
 
-        ready = [product(y) for y in ys[:AHEAD]]
-        for k, y in enumerate(ys):
-            if k + AHEAD < len(ys):
-                ready.append(product(ys[k + AHEAD]))
+        ready = [product(job) for job in jobs[:AHEAD]]
+        for k, (y, layer) in enumerate(jobs):
+            if k + AHEAD < len(jobs):
+                ready.append(product(jobs[k + AHEAD]))
             inside = ready.pop(0)
             for at in range(0, points, ROWS):
                 sum_w = sum_s = None
@@ -194,14 +195,14 @@
                 total_w[place] = sum_w
                 total_s[place] = sum_s
 
-    def own_layer(x, ys):
-        row_sums(x, ys, 0)
+    across_ply = [(y, 1) for y in range(along)]
+    whole = [(y, 0) for y in range(along)]
 
     def inner_row(x, carry):
-        own_layer(x, range(1, along - 1))
-        return carry
-
-    lax.fori_loop(1, across - 1, inner_row, 0)
+        row_sums(x, whole[1:-1])
+        return carry
+
+    lax.fori_loop(1, across - 1, inner_row, 0, unroll=2)
 
     for which in order:
         layer, dx, dy = listed[which]
@@ -238,21 +239,15 @@
     lax.fori_loop(0, 2, halo_end, 0, unroll=2)
 
     def edge_row(x, carry):
-        own_layer(x, (0, along - 1))
+        row_sums(x, [whole[0], whole[-1]] + across_ply)
         return carry
 
     def end_row(end, carry):
-        own_layer(end * (across - 1), range(along))
+        row_sums(end * (across - 1), whole + across_ply)
         return carry
 
     lax.fori_loop(1, across - 1, edge_row, 0)
     lax.fori_loop(0, 2, end_row, 0)
-
-    def other_layer(x, carry):
-        row_sums(x, range(along), 1)
-        return carry
-
-    lax.fori_loop(0, across, other_layer, 0)
 
     ones = jnp.ones((8, 2 * points), jnp.bfloat16)
 

time: 30.4 us -> 29.8 us (0.980)
  Pallas kernels: 28.2 us -> 27.5 us
    pallas_call x1, Pallas kernels: 28.2 us -> 27.5 us  [on_device(): pl.pallas_call(functools.partial(average_kernel, sizes), out_shape=jax.Sh...]
where the time goes in v8:
time: 29.8 us; the launch traced here: 29.6 us
  Pallas kernels  27.5 us (92%)
  other arithmetic  1.39 us (5%)
  between operations  0.66 us (2%)
    pallas_call x1, Pallas kernels, on_device(): pl.pallas_call(functools.partial(average_kernel, sizes), out_shape=jax.Sh...  27.5 us
    select_n x1, other arithmetic, on_device(): jnp.where(scaled < 0.0, 0.0, 1.0 - jnp.exp(-(kappa_new - 1.0) / 2.5) / ka...  1.39 us

profile of v8, /device:TPU:0, one launch (start us, length us, event | category | flops | bytes accessed | tf_op | source)
XLA Modules:
  0.0 29.6 jit_solution(11377944131062981058)
XLA Ops:
  0.6 0.0 copy-start
  0.6 27.5 %shard_map.68 = f32[6,6,1,128]{3,2,1,0:T(1,128)} custom-call(s32[6,1,6]{2,1,0:T(1,128)} %bitcast.11, s32[6,6,1,26]{3,2,1,0:T(1,128)} %bitcast.9, f32[3,6,6,1,128]{4,3,2,1,0:T(1,128)} %bitcast.8, f32[6,6,1,128]{3,2,1,0:T(1,128)} %bitcast.10), custom_call_target="tpu_custom_call" | custom-call | tf_op jit(solution)/shard_map/pallas_call | solution.py:316
  28.2 0.0 copy-done
  28.2 1.4 %compare_select_fusion = (f32[1,6,6,128]{3,0,2,1:T(1,128)}, f32[1,6,6,128]{3,0,2,1:T(1,128)}) fusion(f32[6,6,1,128]{3,2,1,0:T(1,128)} %shard_map.68, f32[1,6,6,128]{3,0,2,1:T(1,128)S(1)} %copy-done), kind=kLoop, calls=%fused_computation | loop fusion | flops 36864 | bytes 73728 | tf_op jit(solution)/shard_map/jit(_where)/select_n | solution.py:348
Async XLA Ops:
  0.6 27.6 %copy-start = (f32[1,6,6,128]{3,0,2,1:T(1,128)S(1)}, f32[1,6,6,128]{3,0,2,1:T(1,128)}, u32[]{:S(2)}) copy-start(f32[1,6,6,128]{3,0,2,1:T(1,128)} %param.7) | copy-start | bytes 55300
